TPU v7x, 256 devices: a whole 4x4x8 slice. The times are simulated.
256 devices in a mesh: seq: 64 (over z, x, core), head: 4 (over y).
Axes of the slice: x: 4, y: 4, z: 8, core: 2. Of those that a mesh axis runs over, the one named last changes fastest.
Arguments:
- queries: bfloat16 [32768, 4096], P('seq', 'head'), may hold values from -200 to 200
- key_rows: bfloat16 [32768, 1024], P('seq', 'head'), may hold values from -6 to 6
- value_rows: bfloat16 [32768, 1024], P('seq', 'head'), may hold values from -6 to 6
- doc_lengths: int32 [64], replicated, may hold values from 1 to 3584, as said below
- block_plan: int32 [256], P('seq'), may hold values from 0 to 255, as said below
- out_weight: bfloat16 [4096, 4096], P('head'), may hold values from -0.125 to 0.125
Outputs:
- projected: bfloat16 [32768, 4096], P('seq', 'head')
Inputs may be any that keep to these rules, and one draw needn't show every extreme that they name: `doc_lengths`: the lengths sum to 32768; the largest is exactly 3584. `block_plan`: every block number occurs once. The 4 entries of index i of seq hold first 2 blocks of index i itself in increasing order, then, in increasing order, the blocks of index i XOR 32 that are not among that index's own first 2 entries.
All inputs are finite; a program needn't handle non-finite values.
Results may differ from a plain program's by a relative error of at most 0.014.
Values may be sent and summed in bfloat16 or wider, within the bound.
A program may use at most 128 MiB of HBM per device.

v0:
```python
import jax
import jax.numpy as jnp
from jax import lax
from jax.sharding import PartitionSpec as P

HEAD_DIM = 128
BLOCKS_DEV = 4
KEPT = 2
REACH = 8
BLOCK = 128


NEG = -1e30


def passed_along(block, axis, distance):
    devices = range(lax.axis_size(axis))
    route = [(i - distance, i) for i in devices if i - distance in devices]
    return lax.ppermute(block, axis, route)


def partner(block, axis, stride):
    count = lax.axis_size(axis)
    route = []
    for low in range(count):
        high = low | 1 << stride
        if high != low and high < count:
            route += [(low, high), (high, low)]
    return lax.ppermute(block, axis, route)


def doc_starts(doc_lengths, positions):
    doc_ends = jnp.cumsum(doc_lengths)
    doc_begins = doc_ends - doc_lengths
    inside = doc_begins[None, :] <= positions[:, None]
    return jnp.max(jnp.where(inside, doc_begins[None, :], 0), axis=1)


def attend(query_rows, query_pos, window_keys, window_values, window_base, doc_lengths):
    row_count = query_rows.shape[0]
    kv_count = window_keys.shape[2] // HEAD_DIM
    group_size = query_rows.shape[1] // HEAD_DIM // kv_count
    tile_width = window_keys.shape[1]
    grouped = query_rows.reshape(row_count, kv_count, group_size, HEAD_DIM)
    query_start = doc_starts(doc_lengths, query_pos)
    lowest = jnp.min(query_start)
    highest = jnp.max(query_pos)
    score_scale = HEAD_DIM ** (-0.5)

    def visit(tile_index, carried):
        key_pos = window_base + tile_index * tile_width + jnp.arange(tile_width, dtype=jnp.int32)
        needed = jnp.logical_and(key_pos[tile_width - 1] >= lowest, key_pos[0] <= highest)

        def compute(current):
            running_max, running_sum, weighted = current
            key_tile = window_keys[tile_index].reshape(tile_width, kv_count, HEAD_DIM)
            value_tile = window_values[tile_index].reshape(tile_width, kv_count, HEAD_DIM)
            scores = (
                jnp.einsum("tgrd,ugd->grtu", grouped, key_tile, preferred_element_type=jnp.float32)
                * score_scale
            )
            allowed = jnp.logical_and(
                key_pos[None, :] >= query_start[:, None], key_pos[None, :] <= query_pos[:, None]
            )
            masked = jnp.where(allowed, scores, NEG)
            new_max = jnp.maximum(running_max, jnp.max(masked, axis=3))
            weights = jnp.where(allowed, jnp.exp(masked - new_max[..., None]), 0.0)
            rescale = jnp.exp(running_max - new_max)
            added = jnp.einsum(
                "grtu,ugd->grtd",
                weights.astype(jnp.bfloat16),
                value_tile,
                preferred_element_type=jnp.float32,
            )
            weighted = weighted * rescale[..., None] + added
            running_sum = running_sum * rescale + jnp.sum(weights, axis=3)
            return (new_max, running_sum, weighted)

        return lax.cond(needed, compute, lambda current: current, carried)

    initial = (
        jnp.full((kv_count, group_size, row_count), NEG, jnp.float32),
        jnp.zeros((kv_count, group_size, row_count), jnp.float32),
        jnp.zeros((kv_count, group_size, row_count, HEAD_DIM), jnp.float32),
    )
    running_max, running_sum, weighted = lax.fori_loop(0, window_keys.shape[0], visit, initial)
    normed = weighted / running_sum[..., None]
    normed = jnp.transpose(normed, (2, 0, 1, 3)).reshape(
        row_count, kv_count * group_size * HEAD_DIM
    )
    return normed.astype(jnp.bfloat16)


def project_heads(heads_out, out_weight):
    partial_value = lax.dot_general(
        out_weight, heads_out, (((0,), (1,)), ((), ())), preferred_element_type=jnp.float32
    )
    summed = lax.psum_scatter(
        lax.optimization_barrier(partial_value.astype(jnp.bfloat16))
        .astype(jnp.float32)
        .astype(jnp.bfloat16),
        "head",
        scatter_dimension=0,
        tiled=True,
    ).astype(jnp.float32)
    return summed.T.astype(jnp.bfloat16)


def local(queries, key_rows, value_rows, doc_lengths, block_plan, out_weight):
    seq_devices = lax.axis_size("seq")
    this_index = lax.axis_index("seq")
    tokens = queries.shape[0]
    key_list = []
    value_list = []
    for offset in range(REACH - 1, 0, -1):
        got_keys, got_values = passed_along((key_rows, value_rows), "seq", offset)
        key_list.append(got_keys)
        value_list.append(got_values)
    window_keys = jnp.stack(key_list + [key_rows], axis=0)
    window_values = jnp.stack(value_list + [value_rows], axis=0)
    window_base = (this_index - REACH + 1) * tokens
    kept_ids = block_plan[:KEPT] - this_index * BLOCKS_DEV
    slot_ids = jnp.arange(BLOCKS_DEV, dtype=jnp.int32)
    is_kept = jnp.sum((slot_ids[:, None] == kept_ids[None, :]).astype(jnp.int32), axis=1)
    moved_ids = jnp.argsort(is_kept, stable=True)[: BLOCKS_DEV - KEPT]
    partner_bit = seq_devices.bit_length() - 2
    home_pos = this_index * tokens + jnp.arange(tokens, dtype=jnp.int32)
    attended = attend(queries, home_pos, window_keys, window_values, window_base, doc_lengths)
    attended = attended.reshape(BLOCKS_DEV, BLOCK, attended.shape[1])
    returned = partner(attended[moved_ids], "seq", partner_bit)
    heads_out = jnp.concatenate([attended[kept_ids], returned], axis=0).reshape(
        tokens, attended.shape[2]
    )
    return project_heads(heads_out, out_weight)


def solution(mesh):
    return jax.shard_map(
        local,
        mesh=mesh,
        in_specs=(
            P("seq", "head"),
            P("seq", "head"),
            P("seq", "head"),
            P(),
            P("seq"),
            P("head", None),
        ),
        out_specs=P("seq", "head"),
        check_vma=False,
    )
```

profile of v0, /device:TPU:1, one launch (start us, length us, event | category | flops | bytes accessed | tf_op | source)
XLA Modules:
  0.0 265.1 jit_solution(9275998108373249663)
XLA Ops:
  6.5 1.1 copy.45
  7.6 5.6 %collective-permute-start.7 = (bf16[512,256]{0,1:T(8,128)(2,1)S(1)}, bf16[512,256]{0,1:T(8,128)(2,1)}, u32[]{:S(2)}, u32[]{:S(2)}) collective-permute-start(bf16[512,256]{0,1:T(8,128)(2,1)S(1)} %copy.45), channel_id=1, source_target_pairs={{0,28},{4,32},{8,36},{12,40},{16,44},{20,48},{24,52},{28,56},{32,6... | collective-permute-start | bytes 786440 | tf_op jit(solution)/shard_map/ppermute | solution.py:19
  13.3 4.4 %collective-permute-start.8 = (bf16[512,256]{0,1:T(8,128)(2,1)S(1)}, bf16[512,256]{0,1:T(8,128)(2,1)}, u32[]{:S(2)}, u32[]{:S(2)}) collective-permute-start(bf16[512,256]{0,1:T(8,128)(2,1)S(1)} %copy.45), channel_id=1, source_target_pairs={{0,24},{4,28},{8,32},{12,36},{16,40},{20,44},{24,48},{28,52},{32,5... | collective-permute-start | bytes 786440 | tf_op jit(solution)/shard_map/ppermute | solution.py:19
  17.7 3.1 %collective-permute-start.9 = (bf16[512,256]{0,1:T(8,128)(2,1)S(1)}, bf16[512,256]{0,1:T(8,128)(2,1)S(1)}, u32[]{:S(2)}, u32[]{:S(2)}) collective-permute-start(bf16[512,256]{0,1:T(8,128)(2,1)S(1)} %copy.45), channel_id=1, source_target_pairs={{0,20},{4,24},{8,28},{12,32},{16,36},{20,40},{24,44},{28,48},{32,5... | collective-permute-start | bytes 786440 | tf_op jit(solution)/shard_map/ppermute | solution.py:19
  20.8 4.4 %collective-permute-start.10 = (bf16[512,256]{0,1:T(8,128)(2,1)S(1)}, bf16[512,256]{0,1:T(8,128)(2,1)S(1)}, u32[]{:S(2)}, u32[]{:S(2)}) collective-permute-start(bf16[512,256]{0,1:T(8,128)(2,1)S(1)} %copy.45), channel_id=1, source_target_pairs={{0,16},{4,20},{8,24},{12,28},{16,32},{20,36},{24,40},{28,44},{32,4... | collective-permute-start | bytes 786440 | tf_op jit(solution)/shard_map/ppermute | solution.py:19
  25.1 4.3 %collective-permute-start.11 = (bf16[512,256]{0,1:T(8,128)(2,1)S(1)}, bf16[512,256]{0,1:T(8,128)(2,1)S(1)}, u32[]{:S(2)}, u32[]{:S(2)}) collective-permute-start(bf16[512,256]{0,1:T(8,128)(2,1)S(1)} %copy.45), channel_id=1, source_target_pairs={{0,12},{4,16},{8,20},{12,24},{16,28},{20,32},{24,36},{28,40},{32,4... | collective-permute-start | bytes 786440 | tf_op jit(solution)/shard_map/ppermute | solution.py:19
  29.5 0.7 compare_select_fusion.1
  30.3 0.7 sort.17
  31.0 0.7 copy.35
  32.0 0.7 sub.21
  32.7 0.6 fusion.16
  33.4 1.1 copy.36
  34.5 1.5 copy.44
  36.0 0.7 copy.53
  36.6 0.7 reduce_min.9
  37.4 2.5 collective-permute-start.12
  39.9 1.0 bitcast_dynamic-update-slice_fusion.7
  40.8 2.8 %collective-permute-start.13 = (bf16[512,256]{0,1:T(8,128)(2,1)S(1)}, bf16[512,256]{0,1:T(8,128)(2,1)S(1)}, u32[]{:S(2)}, u32[]{:S(2)}) collective-permute-start(bf16[512,256]{0,1:T(8,128)(2,1)S(1)} %copy.45), channel_id=1, source_target_pairs={{0,4},{4,8},{8,12},{12,16},{16,20},{20,24},{24,28},{28,32},{32,36}... | collective-permute-start | bytes 786440 | tf_op jit(solution)/shard_map/ppermute | solution.py:19
  43.6 1.0 bitcast_dynamic-update-slice_fusion.6
  44.6 4.3 %collective-permute-start = (bf16[512,256]{0,1:T(8,128)(2,1)S(1)}, bf16[512,256]{0,1:T(8,128)(2,1)S(1)}, u32[]{:S(2)}, u32[]{:S(2)}) collective-permute-start(bf16[512,256]{0,1:T(8,128)(2,1)S(1)} %copy.36), channel_id=1, source_target_pairs={{0,28},{4,32},{8,36},{12,40},{16,44},{20,48},{24,52},{28,56},{32,6... | collective-permute-start | bytes 786440 | tf_op jit(solution)/shard_map/ppermute | solution.py:19
  48.9 4.4 %collective-permute-start.1 = (bf16[512,256]{0,1:T(8,128)(2,1)S(1)}, bf16[512,256]{0,1:T(8,128)(2,1)S(1)}, u32[]{:S(2)}, u32[]{:S(2)}) collective-permute-start(bf16[512,256]{0,1:T(8,128)(2,1)S(1)} %copy.36), channel_id=1, source_target_pairs={{0,24},{4,28},{8,32},{12,36},{16,40},{20,44},{24,48},{28,52},{32,5... | collective-permute-start | bytes 786440 | tf_op jit(solution)/shard_map/ppermute | solution.py:19
  53.4 4.2 %collective-permute-start.2 = (bf16[512,256]{0,1:T(8,128)(2,1)S(1)}, bf16[512,256]{0,1:T(8,128)(2,1)S(1)}, u32[]{:S(2)}, u32[]{:S(2)}) collective-permute-start(bf16[512,256]{0,1:T(8,128)(2,1)S(1)} %copy.36), channel_id=1, source_target_pairs={{0,20},{4,24},{8,28},{12,32},{16,36},{20,40},{24,44},{28,48},{32,5... | collective-permute-start | bytes 786440 | tf_op jit(solution)/shard_map/ppermute | solution.py:19
  57.7 3.2 %collective-permute-start.3 = (bf16[512,256]{0,1:T(8,128)(2,1)S(1)}, bf16[512,256]{0,1:T(8,128)(2,1)S(1)}, u32[]{:S(2)}, u32[]{:S(2)}) collective-permute-start(bf16[512,256]{0,1:T(8,128)(2,1)S(1)} %copy.36), channel_id=1, source_target_pairs={{0,16},{4,20},{8,24},{12,28},{16,32},{20,36},{24,40},{28,44},{32,4... | collective-permute-start | bytes 786440 | tf_op jit(solution)/shard_map/ppermute | solution.py:19
  60.9 3.5 %collective-permute-start.4 = (bf16[512,256]{0,1:T(8,128)(2,1)S(1)}, bf16[512,256]{0,1:T(8,128)(2,1)S(1)}, u32[]{:S(2)}, u32[]{:S(2)}) collective-permute-start(bf16[512,256]{0,1:T(8,128)(2,1)S(1)} %copy.36), channel_id=1, source_target_pairs={{0,12},{4,16},{8,20},{12,24},{16,28},{20,32},{24,36},{28,40},{32,4... | collective-permute-start | bytes 786440 | tf_op jit(solution)/shard_map/ppermute | solution.py:19
  64.6 1.8 collective-permute-start.5
  66.4 0.7 bitcast_dynamic-update-slice_fusion.15
  67.1 3.1 %collective-permute-done.1 = bf16[512,256]{0,1:T(8,128)(2,1)S(1)} collective-permute-done((bf16[512,256]{0,1:T(8,128)(2,1)S(1)}, bf16[512,256]{0,1:T(8,128)(2,1)S(1)}, u32[]{:S(2)}, u32[]{:S(2)}) %collective-permute-start.1) | collective-permute-done | bytes 262176 | tf_op jit(solution)/shard_map/ppermute | solution.py:19
  70.2 1.9 collective-permute-start.6
  72.1 0.7 bitcast_dynamic-update-slice_fusion.14
  72.8 1.0 collective-permute-done.2
  73.8 0.7 bitcast_dynamic-update-slice_fusion.13
  74.6 0.7 bitcast_dynamic-update-slice_fusion.12
  75.3 0.7 bitcast_dynamic-update-slice_fusion.11
  76.0 1.6 collective-permute-done.5
  77.6 0.7 bitcast_dynamic-update-slice_fusion.10
  78.3 2.7 %collective-permute-done.6 = bf16[512,256]{0,1:T(8,128)(2,1)S(1)} collective-permute-done((bf16[512,256]{0,1:T(8,128)(2,1)S(1)}, bf16[512,256]{0,1:T(8,128)(2,1)S(1)}, u32[]{:S(2)}, u32[]{:S(2)}) %collective-permute-start.6) | collective-permute-done | bytes 262176 | tf_op jit(solution)/shard_map/ppermute | solution.py:19
  81.1 0.7 bitcast_dynamic-update-slice_fusion.9
  81.8 0.7 bitcast_dynamic-update-slice_fusion.8
  82.7 44.0 %while.18 = (s32[]{:T(128)}, f32[2,4,512]{2,1,0:T(4,128)S(1)}, f32[2,4,512]{2,1,0:T(4,128)S(1)}, f32[2,4,512,128]{3,2,1,0:T(8,128)S(1)}, s32[]{:T(128)}, /*index...) while((s32[]{:T(128)}, f32[2,4,512]{2,1,0:T(4,128)S(1)}, ...), condition=%wide.region_9.10_spmd.clone, body=%wide.region_4.0_spmd.clone.sunk | while | flops 1102849024 | bytes 33307012 | solution.py:86
  82.7 0.6 fusion.24
  85.9 0.6 fusion.24
  89.1 0.6 fusion.24
  92.4 0.6 fusion.24
  95.6 0.6 fusion.24
  98.8 0.6 fusion.24
  102.0 0.6 fusion.24
  105.1 9.2 %conditional.3 = ((f32[2,4,512]{2,1,0:T(4,128)S(1)}, f32[2,4,512]{2,1,0:T(4,128)S(1)}, f32[2,4,512,128]{3,2,1,0:T(8,128)S(1)})) conditional(s32[]{:T(128)} %convert_element_type.58, (f32[2,4,512]{2,1,0:T(4,128)S(1)}, f32[2,4,512]{2,1,0:T(4,128)S(1)}, f32[2,4,512,128]{3,2,1,0:T(8,128)S(1)}) %tuple.52, (s32[512]{0:T(512)S(1)}, s32[512]{0:T(512)S(1)}, ...), branch_computations={%region_5.5_spmd, %region_6.8_spmd} | conditional | flops 1102848512 | bytes 33302602 | solution.py:79
  105.2 1.1 constant_dynamic-slice_fusion
  106.5 2.1 fusion.2
  108.6 2.0 fusion.4
  110.7 3.6 %multiply_add_fusion = f32[2,4,512,128]{3,2,1,0:T(8,128)S(1)} fusion(f32[2,4,512,128]{3,2,1,0:T(8,128)S(1)} %get-tuple-element.230, bf16[512,2,128,1]{0,2,3,1:T(8,128)(2,1)S(1)} %bitcast.82, f32[2,512,512,4]{2,1,3,0:T(8,128)S(1)} %get-tuple-element.340, f32[2,4,512]{2,1,0:T(4,128)S(1)} %max.2, pred[512,512]{0,1:T(8,128)(4,1)S(1)} %compare_and_fusion, ...), kind=kOutput, calls=%fused_computation.10 | convolution fusion | flops 548405248 | bytes 13139968 | tf_op jit(solution)/shard_map/while/body/eval_jaxpr/cond/branch_1_fun/grtu,ugd->grtd/dot_general | solution.py:69
  114.4 0.6 fusion.24
  117.5 9.2 %conditional.3 = ((f32[2,4,512]{2,1,0:T(4,128)S(1)}, f32[2,4,512]{2,1,0:T(4,128)S(1)}, f32[2,4,512,128]{3,2,1,0:T(8,128)S(1)})) conditional(s32[]{:T(128)} %convert_element_type.58, (f32[2,4,512]{2,1,0:T(4,128)S(1)}, f32[2,4,512]{2,1,0:T(4,128)S(1)}, f32[2,4,512,128]{3,2,1,0:T(8,128)S(1)}) %tuple.52, (s32[512]{0:T(512)S(1)}, s32[512]{0:T(512)S(1)}, ...), branch_computations={%region_5.5_spmd, %region_6.8_spmd} | conditional | flops 1102848512 | bytes 33302602 | solution.py:79
  117.5 1.1 constant_dynamic-slice_fusion
  118.9 2.1 fusion.2
  121.0 2.0 fusion.4
  123.1 3.6 %multiply_add_fusion = f32[2,4,512,128]{3,2,1,0:T(8,128)S(1)} fusion(f32[2,4,512,128]{3,2,1,0:T(8,128)S(1)} %get-tuple-element.230, bf16[512,2,128,1]{0,2,3,1:T(8,128)(2,1)S(1)} %bitcast.82, f32[2,512,512,4]{2,1,3,0:T(8,128)S(1)} %get-tuple-element.340, f32[2,4,512]{2,1,0:T(4,128)S(1)} %max.2, pred[512,512]{0,1:T(8,128)(4,1)S(1)} %compare_and_fusion, ...), kind=kOutput, calls=%fused_computation.10 | convolution fusion | flops 548405248 | bytes 13139968 | tf_op jit(solution)/shard_map/while/body/eval_jaxpr/cond/branch_1_fun/grtu,ugd->grtd/dot_general | solution.py:69
  126.7 0.7 fusion.14
  127.5 0.8 copy.54
  128.3 0.8 convert_element_type.38
  129.6 50.6 %collective-permute-start.14 = (bf16[2,128,1024]{2,1,0:T(8,128)(2,1)S(1)}, bf16[2,128,1024]{2,1,0:T(8,128)(2,1)S(1)}, u32[]{:S(2)}, u32[]{:S(2)}) collective-permute-start(bf16[2,128,1024]{2,1,0:T(8,128)(2,1)S(1)} %gather_fusion.1), channel_id=1, source_target_pairs={{0,128},{128,0},{4,132},{132,4},{8,136},{136,8},{12,140},{140,12},... | collective-permute-start | bytes 1572872 | tf_op jit(solution)/shard_map/ppermute | solution.py:29
  180.9 6.0 %collective-permute-done.14 = bf16[2,128,1024]{2,1,0:T(8,128)(2,1)S(1)} collective-permute-done((bf16[2,128,1024]{2,1,0:T(8,128)(2,1)S(1)}, bf16[2,128,1024]{2,1,0:T(8,128)(2,1)S(1)}, u32[]{:S(2)}, u32[]{:S(2)}) %collective-permute-start.14) | collective-permute-done | bytes 524320 | tf_op jit(solution)/shard_map/ppermute | solution.py:29
  187.0 9.4 %fusion.13 = bf16[4096,512]{0,1:T(8,128)(2,1)} fusion(bf16[512,1024]{1,0:T(8,128)(2,1)S(1)} %bitcast.86, bf16[1024,4096]{1,0:T(8,128)(2,1)} %param.15), kind=kOutput, calls=%fused_computation.22 | convolution fusion | flops 4297064448 | bytes 13631488 | tf_op jit(solution)/shard_map/dot_general | solution.py:95
  196.4 61.9 %reduce-scatter.2.cloned.1.call-done = bf16[1024,512]{0,1:T(8,128)(2,1)} async-done(((bf16[4096,512]{0,1:T(8,128)(2,1)}), bf16[1024,512]{0,1:T(8,128)(2,1)}) %reduce-scatter.2.cloned.1.call-update) | async-done | bytes 1048592 | tf_op jit(solution)/shard_map/reduce_scatter | solution.py:98
  (67 shorter events, 2.7 us)
Async XLA Ops:
  6.5 251.8 %reduce-scatter.2.cloned.1.call-start = ((), (), s32[]{:S(2)}) async-start(), calls=%async_computation.1 | async-start | bytes 5242880 | tf_op jit(solution)/shard_map/reduce_scatter | solution.py:98
  7.6 29.7 %collective-permute-start.7 = (bf16[512,256]{0,1:T(8,128)(2,1)S(1)}, bf16[512,256]{0,1:T(8,128)(2,1)}, u32[]{:S(2)}, u32[]{:S(2)}) collective-permute-start(bf16[512,256]{0,1:T(8,128)(2,1)S(1)} %copy.45), channel_id=1, source_target_pairs={{0,28},{4,32},{8,36},{12,40},{16,44},{20,48},{24,52},{28,56},{32,6... | collective-permute-start | bytes 786440 | tf_op jit(solution)/shard_map/ppermute | solution.py:19
  13.3 27.6 %collective-permute-start.8 = (bf16[512,256]{0,1:T(8,128)(2,1)S(1)}, bf16[512,256]{0,1:T(8,128)(2,1)}, u32[]{:S(2)}, u32[]{:S(2)}) collective-permute-start(bf16[512,256]{0,1:T(8,128)(2,1)S(1)} %copy.45), channel_id=1, source_target_pairs={{0,24},{4,28},{8,32},{12,36},{16,40},{20,44},{24,48},{28,52},{32,5... | collective-permute-start | bytes 786440 | tf_op jit(solution)/shard_map/ppermute | solution.py:19
  17.7 26.9 %collective-permute-start.9 = (bf16[512,256]{0,1:T(8,128)(2,1)S(1)}, bf16[512,256]{0,1:T(8,128)(2,1)S(1)}, u32[]{:S(2)}, u32[]{:S(2)}) collective-permute-start(bf16[512,256]{0,1:T(8,128)(2,1)S(1)} %copy.45), channel_id=1, source_target_pairs={{0,20},{4,24},{8,28},{12,32},{16,36},{20,40},{24,44},{28,48},{32,5... | collective-permute-start | bytes 786440 | tf_op jit(solution)/shard_map/ppermute | solution.py:19
  20.8 28.2 %collective-permute-start.10 = (bf16[512,256]{0,1:T(8,128)(2,1)S(1)}, bf16[512,256]{0,1:T(8,128)(2,1)S(1)}, u32[]{:S(2)}, u32[]{:S(2)}) collective-permute-start(bf16[512,256]{0,1:T(8,128)(2,1)S(1)} %copy.45), channel_id=1, source_target_pairs={{0,16},{4,20},{8,24},{12,28},{16,32},{20,36},{24,40},{28,44},{32,4... | collective-permute-start | bytes 786440 | tf_op jit(solution)/shard_map/ppermute | solution.py:19
  25.1 28.3 %collective-permute-start.11 = (bf16[512,256]{0,1:T(8,128)(2,1)S(1)}, bf16[512,256]{0,1:T(8,128)(2,1)S(1)}, u32[]{:S(2)}, u32[]{:S(2)}) collective-permute-start(bf16[512,256]{0,1:T(8,128)(2,1)S(1)} %copy.45), channel_id=1, source_target_pairs={{0,12},{4,16},{8,20},{12,24},{16,28},{20,32},{24,36},{28,40},{32,4... | collective-permute-start | bytes 786440 | tf_op jit(solution)/shard_map/ppermute | solution.py:19
  37.4 20.3 %collective-permute-start.12 = (bf16[512,256]{0,1:T(8,128)(2,1)S(1)}, bf16[512,256]{0,1:T(8,128)(2,1)S(1)}, u32[]{:S(2)}, u32[]{:S(2)}) collective-permute-start(bf16[512,256]{0,1:T(8,128)(2,1)S(1)} %copy.45), channel_id=1, source_target_pairs={{0,8},{4,12},{8,16},{12,20},{16,24},{20,28},{24,32},{28,36},{32,40... | collective-permute-start | bytes 786440 | tf_op jit(solution)/shard_map/ppermute | solution.py:19
  40.8 20.1 %collective-permute-start.13 = (bf16[512,256]{0,1:T(8,128)(2,1)S(1)}, bf16[512,256]{0,1:T(8,128)(2,1)S(1)}, u32[]{:S(2)}, u32[]{:S(2)}) collective-permute-start(bf16[512,256]{0,1:T(8,128)(2,1)S(1)} %copy.45), channel_id=1, source_target_pairs={{0,4},{4,8},{8,12},{12,16},{16,20},{20,24},{24,28},{28,32},{32,36}... | collective-permute-start | bytes 786440 | tf_op jit(solution)/shard_map/ppermute | solution.py:19
  44.6 19.9 %collective-permute-start = (bf16[512,256]{0,1:T(8,128)(2,1)S(1)}, bf16[512,256]{0,1:T(8,128)(2,1)S(1)}, u32[]{:S(2)}, u32[]{:S(2)}) collective-permute-start(bf16[512,256]{0,1:T(8,128)(2,1)S(1)} %copy.36), channel_id=1, source_target_pairs={{0,28},{4,32},{8,36},{12,40},{16,44},{20,48},{24,52},{28,56},{32,6... | collective-permute-start | bytes 786440 | tf_op jit(solution)/shard_map/ppermute | solution.py:19
  48.9 21.3 %collective-permute-start.1 = (bf16[512,256]{0,1:T(8,128)(2,1)S(1)}, bf16[512,256]{0,1:T(8,128)(2,1)S(1)}, u32[]{:S(2)}, u32[]{:S(2)}) collective-permute-start(bf16[512,256]{0,1:T(8,128)(2,1)S(1)} %copy.36), channel_id=1, source_target_pairs={{0,24},{4,28},{8,32},{12,36},{16,40},{20,44},{24,48},{28,52},{32,5... | collective-permute-start | bytes 786440 | tf_op jit(solution)/shard_map/ppermute | solution.py:19
  53.4 20.4 %collective-permute-start.2 = (bf16[512,256]{0,1:T(8,128)(2,1)S(1)}, bf16[512,256]{0,1:T(8,128)(2,1)S(1)}, u32[]{:S(2)}, u32[]{:S(2)}) collective-permute-start(bf16[512,256]{0,1:T(8,128)(2,1)S(1)} %copy.36), channel_id=1, source_target_pairs={{0,20},{4,24},{8,28},{12,32},{16,36},{20,40},{24,44},{28,48},{32,5... | collective-permute-start | bytes 786440 | tf_op jit(solution)/shard_map/ppermute | solution.py:19
  57.7 16.9 %collective-permute-start.3 = (bf16[512,256]{0,1:T(8,128)(2,1)S(1)}, bf16[512,256]{0,1:T(8,128)(2,1)S(1)}, u32[]{:S(2)}, u32[]{:S(2)}) collective-permute-start(bf16[512,256]{0,1:T(8,128)(2,1)S(1)} %copy.36), channel_id=1, source_target_pairs={{0,16},{4,20},{8,24},{12,28},{16,32},{20,36},{24,40},{28,44},{32,4... | collective-permute-start | bytes 786440 | tf_op jit(solution)/shard_map/ppermute | solution.py:19
  60.9 14.4 %collective-permute-start.4 = (bf16[512,256]{0,1:T(8,128)(2,1)S(1)}, bf16[512,256]{0,1:T(8,128)(2,1)S(1)}, u32[]{:S(2)}, u32[]{:S(2)}) collective-permute-start(bf16[512,256]{0,1:T(8,128)(2,1)S(1)} %copy.36), channel_id=1, source_target_pairs={{0,12},{4,16},{8,20},{12,24},{16,28},{20,32},{24,36},{28,40},{32,4... | collective-permute-start | bytes 786440 | tf_op jit(solution)/shard_map/ppermute | solution.py:19
  64.5 17.2 %copy-start = (bf16[8,512,256]{1,2,0:T(8,128)(2,1)}, bf16[8,512,256]{1,2,0:T(8,128)(2,1)S(1)}, u32[]{:S(2)}) copy-start(bf16[8,512,256]{1,2,0:T(8,128)(2,1)S(1)} %bitcast_dynamic-update-slice_fusion) | copy-start | bytes 6291460
  64.6 13.1 %collective-permute-start.5 = (bf16[512,256]{0,1:T(8,128)(2,1)S(1)}, bf16[512,256]{0,1:T(8,128)(2,1)S(1)}, u32[]{:S(2)}, u32[]{:S(2)}) collective-permute-start(bf16[512,256]{0,1:T(8,128)(2,1)S(1)} %copy.36), channel_id=1, source_target_pairs={{0,8},{4,12},{8,16},{12,20},{16,24},{20,28},{24,32},{28,36},{32,40... | collective-permute-start | bytes 786440 | tf_op jit(solution)/shard_map/ppermute | solution.py:19
  70.2 10.9 %collective-permute-start.6 = (bf16[512,256]{0,1:T(8,128)(2,1)S(1)}, bf16[512,256]{0,1:T(8,128)(2,1)S(1)}, u32[]{:S(2)}, u32[]{:S(2)}) collective-permute-start(bf16[512,256]{0,1:T(8,128)(2,1)S(1)} %copy.36), channel_id=1, source_target_pairs={{0,4},{4,8},{8,12},{12,16},{16,20},{20,24},{24,28},{28,32},{32,36}... | collective-permute-start | bytes 786440 | tf_op jit(solution)/shard_map/ppermute | solution.py:19
  129.6 57.2 %collective-permute-start.14 = (bf16[2,128,1024]{2,1,0:T(8,128)(2,1)S(1)}, bf16[2,128,1024]{2,1,0:T(8,128)(2,1)S(1)}, u32[]{:S(2)}, u32[]{:S(2)}) collective-permute-start(bf16[2,128,1024]{2,1,0:T(8,128)(2,1)S(1)} %gather_fusion.1), channel_id=1, source_target_pairs={{0,128},{128,0},{4,132},{132,4},{8,136},{136,8},{12,140},{140,12},... | collective-permute-start | bytes 1572872 | tf_op jit(solution)/shard_map/ppermute | solution.py:29
Sparse Core Ops, SparseCore 0:
  196.5 61.7 reduce-scatter.1
where the time goes:
time: 266 us; the launch traced here: 265 us
  starting transfers between devices  101 us (38%)
  waiting for transfers between devices  76.4 us (29%)
  local copies, waits for them, and re-layouts  23.2 us (9%)
  matrix products  20.8 us (8%)
  loops' own time  20.6 us (8%)
  between operations  13.7 us (5%)
  other arithmetic  9.35 us (4%)
    reduce_scatter x1, waiting for transfers between devices, project_heads(): lax.psum_scatter(lax.optimization_barrier(partial_value.astype(jnp.bfloat...  61.9 us
    ppermute x1, starting transfers between devices, partner(): return lax.ppermute(block, axis, route)  50.6 us
    ppermute x14, starting transfers between devices, passed_along(): return lax.ppermute(block, axis, route)  50.5 us
    another operation x1, loops' own time, attend(): lax.fori_loop(0, window_keys.shape[0], visit, initial)  20.4 us
    unnamed x20, local copies, waits for them, and re-layouts  11.5 us
    dot_general x1, matrix products, project_heads(): lax.dot_general(out_weight, heads_out, (((0,), (1,)), ((), ())), preferre...  9.38 us
    ppermute x14, waiting for transfers between devices, passed_along(): return lax.ppermute(block, axis, route)  8.43 us
    dot_general x2, matrix products, compute(): jnp.einsum('grtu,ugd->grtd', weights.astype(jnp.bfloat16), value_tile, pr...  7.29 us
  transfers between devices with their start and end apart: 16, of which 6 were waited for; matrix products, arithmetic and copies ran while one was open for 6% of the time, Pallas kernels for 0%

commit v1 on v0

v1 whole, which is shorter than its diff:
```python
import jax
import jax.numpy as jnp
from jax import lax
from jax.experimental import pallas as pl
from jax.experimental.pallas import tpu as pltpu
from jax.sharding import PartitionSpec as P

MESH = pl.DeviceIdType.MESH
F32 = jnp.float32
BF16 = jnp.bfloat16
HEAD_DIM = 128
DOCS = 64
X_CHIPS = 4
Z_CHIPS = 8
CHIPS = X_CHIPS * Z_CHIPS
HEADS = 8
KV = 2
T = 512
BLOCK = 128
WIDE = 1024
HALF = 512
VROWS = HEAD_DIM + 16
EXP_SCALE = 1.4426950408889634 / HEAD_DIM**0.5
BIG = 1e30
OWN, CROSS, NEAR, NEAR_O, FAR, FAR_O, MID, MID_O, ABOVE = range(9)
DUMMY = 8


def transposed(block):
    return block.astype(F32).T.astype(BF16)


def kernel(
    q_hbm, k_hbm, v_hbm, lens, plan, w_hbm, out,
    qv, win, relay, wbuf, ka, vat, qt, m_ref, acc, s0, s1, p0, p1, a0, a1,
    att, keep, sent, landed, res, moved_in,
    in_sem, w_sem, kv_send, kv_recv, y_send, y_recv, z_send, z_recv,
):
    index = lax.axis_index("seq")
    y = lax.axis_index("head")
    core = lax.rem(index, 2)
    chip = index // 2
    x = lax.rem(chip, X_CHIPS)
    z = chip // X_CHIPS

    def at(zz, xx, cc):
        return ((zz * X_CHIPS + xx) * 2 + cc, y)

    z_up = at(lax.rem(z + 1, Z_CHIPS), x, core)
    z_down = at(lax.rem(z + Z_CHIPS - 1, Z_CHIPS), x, core)
    x_up = at(z, lax.rem(x + 1, X_CHIPS), core)
    x_down = at(z, lax.rem(x + X_CHIPS - 1, X_CHIPS), core)
    sibling = at(z, x, 1 - core)
    partner = at(lax.rem(z + Z_CHIPS // 2, Z_CHIPS), x, core)
    y_up = (index, lax.rem(y + 1, 4))
    y_down = (index, lax.rem(y + 3, 4))

    load_k = pltpu.make_async_copy(k_hbm, win.at[OWN, :, pl.ds(0, 256)], in_sem.at[0])
    load_v = pltpu.make_async_copy(v_hbm, win.at[OWN, :, pl.ds(256, 256)], in_sem.at[1])
    load_q = pltpu.make_async_copy(q_hbm, qv, in_sem.at[2])
    load_k.start()
    load_v.start()
    load_q.start()
    load_w = []
    for step in (2, 1, 3, 0):
        group = lax.rem(y + step, 4)
        load_w.append(
            pltpu.make_async_copy(
                w_hbm.at[:, pl.ds(pl.multiple_of(group * WIDE, WIDE), WIDE)], wbuf.at[step], w_sem.at[step]
            )
        )

    barrier = pltpu.get_barrier_semaphore()
    for other in (z_up, z_down, x_up, x_down, sibling, partner, y_up, y_down):
        pl.semaphore_signal(barrier, inc=1, device_id=other, device_id_type=MESH)
    pl.semaphore_wait(barrier, 8)

    def part(ref, half):
        return ref.at[pl.ds(half * 256, 256), :]

    def send(source, slot, half, target):
        return pltpu.make_async_remote_copy(
            src_ref=part(win.at[source], half),
            dst_ref=part(win.at[slot], half),
            send_sem=kv_send.at[slot, half],
            recv_sem=kv_recv.at[slot, half],
            device_id=target,
            device_id_type=MESH,
        )

    def send_relay(source, half, way, target):
        return pltpu.make_async_remote_copy(
            src_ref=part(win.at[source], half),
            dst_ref=relay.at[way],
            send_sem=kv_send.at[9, way],
            recv_sem=kv_recv.at[9, way],
            device_id=target,
            device_id_type=MESH,
        )

    def pass_relay(half, way, target):
        return pltpu.make_async_remote_copy(
            src_ref=relay.at[way],
            dst_ref=part(win.at[MID], half),
            send_sem=kv_send.at[MID, half],
            recv_sem=kv_recv.at[MID, half],
            device_id=target,
            device_id_type=MESH,
        )

    load_k.wait()
    load_v.wait()

    for half in (0, 1):
        send(OWN, ABOVE, half, z_up).start()

        @pl.when(x < 3)
        def _():
            send(OWN, NEAR, half, x_up).start()

        @pl.when(x == 0)
        def _():
            send(OWN, FAR, half, x_down).start()

        @pl.when(core == 0)
        def _():
            send(OWN, CROSS, half, sibling).start()

    @pl.when(x == 1)
    def _():
        send_relay(OWN, 1, 1, x_down).start()

    for copy in load_w:
        copy.start()

    lane = lax.broadcasted_iota(jnp.int32, (1, HEAD_DIM), 1)
    begins = jnp.zeros((1, HEAD_DIM), jnp.int32)
    ends = jnp.zeros((1, HEAD_DIM), jnp.int32)
    for doc in range(DOCS):
        length = lens[doc]
        begins = begins + jnp.where(lane > doc, length, 0)
        ends = ends + jnp.where(lane >= doc, length, 0)
    kept0 = jnp.clip(plan[0] - index * 4, 0, 3)
    kept1 = jnp.clip(plan[1] - index * 4, 0, 3)
    moved0 = jnp.where(kept0 != 0, 0, jnp.where(kept1 != 1, 1, 2))
    moved1 = jnp.clip(6 - kept0 - kept1 - moved0, 0, 3)
    ids = (moved0, moved1, kept0, kept1)

    def same_doc(base, rows):
        pos = base + lax.broadcasted_iota(jnp.int32, (rows, HEAD_DIM), 0)
        return jnp.logical_and(pos >= begins, pos < ends)

    for g in range(2 * 8):
        vat[g, HEAD_DIM:, :] = jnp.ones((VROWS - HEAD_DIM, T), BF16)
    load_q.wait()
    for b in range(4):
        rows = qv[ids[b]]
        marks = jnp.where(same_doc(index * T + ids[b] * BLOCK, BLOCK), 0.0, -BIG).T.astype(BF16)
        for h in range(HEADS):
            c = (b // 2) * 4 + h // 2
            col = (h % 2) * 256 + (b % 2) * BLOCK
            qt[c, :HEAD_DIM, col : col + BLOCK] = transposed(rows[:, h * HEAD_DIM : (h + 1) * HEAD_DIM])
            qt[c, HEAD_DIM:, col : col + BLOCK] = marks
    m_ref[...] = jnp.full(m_ref.shape, -3e38, F32)
    acc[...] = jnp.zeros(acc.shape, F32)

    def prepare(tile, base):
        hot = jnp.where(same_doc(base, T), 1.0, 0.0).astype(BF16)
        for g in range(KV):
            ka[2 * tile + g, :, :HEAD_DIM] = win[tile, :, g * HEAD_DIM : (g + 1) * HEAD_DIM]
            ka[2 * tile + g, :, HEAD_DIM:] = hot
            vat[2 * tile + g, :HEAD_DIM, :] = transposed(win[tile, :, 256 + g * HEAD_DIM : 256 + (g + 1) * HEAD_DIM])

    scores, probs, scales = (s0, s1), (p0, p1), (a0, a1)

    def score(kg, c, which, causal):
        value = jnp.dot(ka[kg], qt[c], preferred_element_type=F32)
        if causal is not None:
            value = jnp.where(causal, value, -BIG)
        scores[which][...] = value

    def soften(c, which):
        value = scores[which][...]
        old = m_ref[c]
        new = jnp.maximum(old, jnp.max(value, axis=0, keepdims=True))
        probs[which][...] = jnp.exp2((value - new) * EXP_SCALE).astype(BF16)
        scales[which][...] = jnp.exp2((old - new) * EXP_SCALE)
        m_ref[c] = new

    def weigh(kg, c, which):
        acc[c] = acc[c] * scales[which][...] + jnp.dot(vat[kg], probs[which][...], preferred_element_type=F32)

    prepare(OWN, index * T)
    lanes = lax.broadcasted_iota(jnp.int32, (T, T), 1)
    key_row = lax.broadcasted_iota(jnp.int32, (T, T), 0)
    inner = lanes % BLOCK
    second = (lanes // BLOCK) % 2
    limits = [inner + BLOCK * jnp.where(second == 0, ids[2 * half], ids[2 * half + 1]) for half in (0, 1)]

    def own_half(half):
        causal = key_row <= limits[half]
        for u in range(4):
            score(u // 2, half * 4 + u, u % 2, causal)
            soften(half * 4 + u, u % 2)
            weigh(u // 2, half * 4 + u, u % 2)

    own_half(0)
    own_half(1)

    for half in (0, 1):
        send(OWN, ABOVE, half, z_up).wait_recv()

        @pl.when(x == 2)
        def _():
            if half == 0:
                send_relay(ABOVE, 0, 0, x_up).start()

        @pl.when(x > 0)
        def _():
            send(ABOVE, FAR, half, x_down).start()

        @pl.when(x == 3)
        def _():
            send(ABOVE, NEAR, half, x_up).start()

        @pl.when(core == 1)
        def _():
            send(ABOVE, CROSS, half, sibling).start()

    @pl.when(x == 0)
    def _():
        send_relay(OWN, 1, 1, x_down).wait_recv()
        pass_relay(1, 1, x_down).start()

    def near_came():
        for half in (0, 1):
            send(OWN, NEAR, half, x_up).wait_recv()
            send(NEAR, NEAR_O, half, sibling).start()
            if half == 0:

                @pl.when(x != 3)
                def _():
                    send(NEAR, MID, 0, x_up).start()

    @pl.when(x != 0)
    def _():
        near_came()

    def came(slot):
        for half in (0, 1):
            send(OWN, slot, half, sibling).wait_recv()

    def far_came():
        for half in (0, 1):
            send(OWN, FAR, half, x_down).wait_recv()
            send(FAR, FAR_O, half, sibling).start()
            if half == 1:

                @pl.when(x != 0)
                def _():
                    send(FAR, MID, 1, x_down).start()

    def mid_came():
        for half in (0, 1):
            send(OWN, MID, half, x_up).wait_recv()
            send(MID, MID_O, half, sibling).start()

    def copy_y(kind, block, way):
        return pltpu.make_async_remote_copy(
            src_ref=sent.at[kind, block, way],
            dst_ref=landed.at[kind, block, way],
            send_sem=y_send.at[kind, block, way],
            recv_sem=y_recv.at[kind, block, way],
            device_id=y_up if way == 0 else y_down,
            device_id_type=MESH,
        )

    def give(kind, block, way, value):
        sent[kind, block, way] = value.astype(BF16)
        copy_y(kind, block, way).start()

    def project(block, step, part_index):
        return jnp.dot(
            att[block], wbuf[step, :, part_index * HALF : (part_index + 1) * HALF], preferred_element_type=F32
        )

    def first_step(block):
        for way in (0, 1):
            give(0, block, way, project(block, 2, way))
        give(1, block, 0, project(block, 1, 1))
        give(1, block, 1, project(block, 3, 0))
        keep[block, 0] = project(block, 1, 0)
        keep[block, 1] = project(block, 3, 1)

    def second_step(block):
        for way in (0, 1):
            copy_y(0, block, way).wait_recv()
            give(2, block, way, keep[block, way] + landed[0, block, way].astype(F32))

    def last_step(block):
        own = [project(block, 0, 0), project(block, 0, 1)]
        for kind, way in ((1, 0), (1, 1), (2, 0), (2, 1)):
            copy_y(kind, block, way).wait_recv()
        left = own[0] + landed[2, block, 0].astype(F32) + landed[1, block, 1].astype(F32)
        right = own[1] + landed[1, block, 0].astype(F32) + landed[2, block, 1].astype(F32)
        return left.astype(BF16), right.astype(BF16)

    def copy_z(block):
        return pltpu.make_async_remote_copy(
            src_ref=res.at[block],
            dst_ref=moved_in.at[block],
            send_sem=z_send.at[block],
            recv_sem=z_recv.at[block],
            device_id=partner,
            device_id_type=MESH,
        )

    def finish_moved(block):
        left, right = last_step(block)
        res[block, :, :HALF] = left
        res[block, :, HALF:] = right
        copy_z(block).start()

    def finish_kept(block):
        left, right = last_step(block)
        out[pl.ds((block - 2) * BLOCK, BLOCK), :HALF] = left
        out[pl.ds((block - 2) * BLOCK, BLOCK), HALF:] = right

    def normalise(half):
        for u in range(4):
            c = half * 4 + u
            value = acc[c]
            rows = (value[:HEAD_DIM] / value[HEAD_DIM : HEAD_DIM + 1]).T.astype(BF16)
            for r in range(2):
                h = u * 2 + r
                for b in range(2):
                    start = r * 256 + b * BLOCK
                    att[half * 2 + b, :, h * HEAD_DIM : (h + 1) * HEAD_DIM] = rows[start : start + BLOCK]

    back = (0, 1, 1, 3, 3, 2, 2)

    def run_half(half, hooks):
        def segment(s, carry):
            tile = s + 1
            for when, hook in hooks.items():
                pl.when(s == when)(hook)
            if half == 0:
                distance = jnp.where(tile >= MID, 2, jnp.where(tile >= FAR, 3, 1))
                side = jnp.where(lax.rem(tile, 2) == 0, core, 1 - core)
                distance = jnp.where(tile == CROSS, jnp.where(core == 0, 4, 0), distance)
                there = lax.rem(chip - distance + CHIPS, CHIPS)
                prepare(tile, (there * 2 + side) * T)
            first = s == 0
            for u in range(4):
                c = half * 4 + u
                score(2 * tile + u // 2, c, u % 2, None)
                soften(c - 1 if u else jnp.where(first, DUMMY, half * 4 + 3), (u + 1) % 2)
                if u >= 2:
                    weigh(2 * tile + (u - 2) // 2, c - 2, u % 2)
                else:
                    weigh(2 * s + 1, jnp.where(first, DUMMY, half * 4 + 2 + u), u % 2)
            return carry

        lax.fori_loop(0, 7, segment, 0)
        soften(half * 4 + 3, 1)
        weigh(15, half * 4 + 2, 0)
        weigh(15, half * 4 + 3, 1)

    def hook_near():
        pl.when(x == 0)(near_came)

    def hook_near_other():
        came(NEAR_O)

        @pl.when(x == 3)
        def _():
            send_relay(OWN, 0, 0, x_up).wait_recv()
            pass_relay(0, 0, x_up).start()

        far_came()

    run_half(
        0,
        {
            0: lambda: came(CROSS),
            1: hook_near,
            2: hook_near_other,
            4: lambda: came(FAR_O),
            5: mid_came,
            6: lambda: came(MID_O),
        },
    )
    normalise(0)
    for copy in load_w:
        copy.wait()
    first_step(0)
    first_step(1)
    run_half(
        1,
        {0: lambda: second_step(0), 2: lambda: second_step(1), 5: lambda: finish_moved(0)},
    )
    normalise(1)
    first_step(2)
    first_step(3)
    finish_moved(1)
    second_step(2)
    second_step(3)
    finish_kept(2)
    finish_kept(3)
    for block in (0, 1):
        copy_z(block).wait_recv()
        out[pl.ds((2 + block) * BLOCK, BLOCK), :] = moved_in[block]

    for half in (0, 1):
        for slot in (ABOVE, CROSS, NEAR, NEAR_O, FAR, FAR_O, MID, MID_O):
            send(OWN, slot, half, sibling).wait_send()

    @pl.when(x == 1)
    def _():
        send_relay(OWN, 1, 1, x_down).wait_send()

    @pl.when(x == 2)
    def _():
        send_relay(ABOVE, 0, 0, x_up).wait_send()

    for block in range(4):
        for kind in range(3):
            for way in (0, 1):
                copy_y(kind, block, way).wait_send()
    for block in (0, 1):
        copy_z(block).wait_send()


def local(queries, key_rows, value_rows, doc_lengths, block_plan, out_weight):
    tokens, width = queries.shape
    anywhere = pl.BlockSpec(memory_space=pl.ANY)
    scalars = pl.BlockSpec(memory_space=pltpu.SMEM)
    return pl.pallas_call(
        kernel,
        out_shape=jax.ShapeDtypeStruct((tokens, width), BF16),
        in_specs=[anywhere, anywhere, anywhere, scalars, scalars, anywhere],
        out_specs=pl.BlockSpec(memory_space=pltpu.VMEM),
        scratch_shapes=[
            pltpu.VMEM((4, BLOCK, width), BF16),
            pltpu.VMEM((9, T, 512), BF16),
            pltpu.VMEM((2, 256, 512), BF16),
            pltpu.VMEM((4, WIDE, WIDE), BF16),
            pltpu.VMEM((16, T, 256), BF16),
            pltpu.VMEM((16, VROWS, T), BF16),
            pltpu.VMEM((8, 256, T), BF16),
            pltpu.VMEM((9, 1, T), F32),
            pltpu.VMEM((9, VROWS, T), F32),
            pltpu.VMEM((T, T), F32),
            pltpu.VMEM((T, T), F32),
            pltpu.VMEM((T, T), BF16),
            pltpu.VMEM((T, T), BF16),
            pltpu.VMEM((1, T), F32),
            pltpu.VMEM((1, T), F32),
            pltpu.VMEM((4, BLOCK, WIDE), BF16),
            pltpu.VMEM((4, 2, BLOCK, HALF), F32),
            pltpu.VMEM((3, 4, 2, BLOCK, HALF), BF16),
            pltpu.VMEM((3, 4, 2, BLOCK, HALF), BF16),
            pltpu.VMEM((2, BLOCK, WIDE), BF16),
            pltpu.VMEM((2, BLOCK, WIDE), BF16),
            pltpu.SemaphoreType.DMA((3,)),
            pltpu.SemaphoreType.DMA((4,)),
            pltpu.SemaphoreType.DMA((10, 2)),
            pltpu.SemaphoreType.DMA((10, 2)),
            pltpu.SemaphoreType.DMA((3, 4, 2)),
            pltpu.SemaphoreType.DMA((3, 4, 2)),
            pltpu.SemaphoreType.DMA((2,)),
            pltpu.SemaphoreType.DMA((2,)),
        ],
        compiler_params=pltpu.CompilerParams(
            collective_id=0, has_side_effects=True, vmem_limit_bytes=56 << 20
        ),
        name="attend_and_project",
    )(queries.reshape(4, BLOCK, width), key_rows, value_rows, doc_lengths, block_plan, out_weight)


def solution(mesh):
    return jax.shard_map(
        local,
        mesh=mesh,
        in_specs=(
            P("seq", "head"),
            P("seq", "head"),
            P("seq", "head"),
            P(),
            P("seq"),
            P("head", None),
        ),
        out_specs=P("seq", "head"),
        check_vma=False,
    )
```

time: 266 us -> 91.3 us (0.34)
  starting transfers between devices: 101 us -> 0 us
  Pallas kernels: 0 us -> 88.8 us
  waiting for transfers between devices: 76.4 us -> 0 us
  local copies, waits for them, and re-layouts: 23.2 us -> 2.26 us
  matrix products: 20.8 us -> 0 us
  loops' own time: 20.6 us -> 0 us
  between operations: 13.7 us -> 0.01 us
  other arithmetic: 9.35 us -> 0 us
    ppermute x15 -> x0, starting transfers between devices: 101 us -> none  [the longest x1 50.6 us: partner(): return lax.ppermute(block, axis, route)]
    pallas_call x0 -> x1, Pallas kernels: none -> 88.8 us  [local(): pl.pallas_call(kernel, out_shape=jax.ShapeDtypeStruct((tokens, width), BF...]
    reduce_scatter x1 -> x0, waiting for transfers between devices: 61.9 us -> none  [project_heads(): lax.psum_scatter(lax.optimization_barrier(partial_value.astype(jnp.bfloat...]
    dot_general x5 -> x0, matrix products: 20.8 us -> none  [the longest x1 9.38 us: project_heads(): lax.dot_general(out_weight, heads_out, (((0,), (1,)), ((), ())), preferre...]
    another operation x9 -> x0, loops' own time: 20.6 us -> none  [the longest x1 20.4 us: attend(): lax.fori_loop(0, window_keys.shape[0], visit, initial)]
    ppermute x15 -> x0, waiting for transfers between devices: 14.4 us -> none  [the longest x14 8.43 us: passed_along(): return lax.ppermute(block, axis, route)]
    unnamed x20 -> x1, local copies, waits for them, and re-layouts: 11.5 us -> 2.26 us
    slice x8 -> x0, local copies, waits for them, and re-layouts: 5.19 us -> none  [visit(): key_pos[0] <= highest]
  transfers between devices with their start and end apart: 16 -> 0, of which waited for: 6 -> 0; matrix products, arithmetic and copies ran while one was open for 6% -> 0% of each run, Pallas kernels for 0% -> 0%
where the time goes in v1:
time: 91.3 us; the launch traced here: 91.1 us
  Pallas kernels  88.8 us (97%)
  local copies, waits for them, and re-layouts  2.26 us (2%)
    pallas_call x1, Pallas kernels, local(): pl.pallas_call(kernel, out_shape=jax.ShapeDtypeStruct((tokens, width), BF...  88.8 us
    unnamed x1, local copies, waits for them, and re-layouts  2.26 us

profile of v1, /device:TPU:1, one launch (start us, length us, event | category | flops | bytes accessed | tf_op | source)
XLA Modules:
  0.0 91.1 jit_solution(17254015695363170768)
XLA Ops:
  0.0 88.8 %attend_and_project.1 = bf16[512,1024]{1,0:T(8,128)(2,1)} custom-call(bf16[4,128,1024]{2,1,0:T(8,128)(2,1)} %bitcast.1, bf16[512,256]{1,0:T(8,128)(2,1)} %k_hbm.1, bf16[512,256]{1,0:T(8,128)(2,1)} %v_hbm.1, s32[64]{0:T(128)} %lens.1, s32[4]{0:T(128)} %plan.1, bf16[1024,4096]{1,0:T(8,128)(2,1)} %w_hbm.1), custom_call_target="tpu_custom_call" | custom-call | tf_op jit(solution)/shard_map/attend_and_project/pallas_call | solution.py:438
  88.9 2.3 %copy.8 = bf16[512,1024]{1,0:T(8,128)(2,1)} copy(bf16[512,1024]{1,0:T(8,128)(2,1)} %attend_and_project.1) | data formatting | bytes 2097152

commit v2 on v1

--- a/solution.py
+++ b/solution.py
@@ -17,6 +17,7 @@
 KV = 2
 T = 512
 BLOCK = 128
+QUARTER = 128
 WIDE = 1024
 HALF = 512
 VROWS = HEAD_DIM + 16
@@ -33,7 +34,7 @@
 def kernel(
     q_hbm, k_hbm, v_hbm, lens, plan, w_hbm, out,
     qv, win, relay, wbuf, ka, vat, qt, m_ref, acc, s0, s1, p0, p1, a0, a1,
-    att, keep, sent, landed, res, moved_in,
+    att, keep, sent, landed, res, midway, moved_in,
     in_sem, w_sem, kv_send, kv_recv, y_send, y_recv, z_send, z_recv,
 ):
     index = lax.axis_index("seq")
@@ -51,7 +52,9 @@
     x_up = at(z, lax.rem(x + 1, X_CHIPS), core)
     x_down = at(z, lax.rem(x + X_CHIPS - 1, X_CHIPS), core)
     sibling = at(z, x, 1 - core)
-    partner = at(lax.rem(z + Z_CHIPS // 2, Z_CHIPS), x, core)
+    way_z = jnp.where(core == 0, 2, Z_CHIPS - 2)
+    onward = at(lax.rem(z + way_z, Z_CHIPS), x, core)
+    behind = at(lax.rem(z + Z_CHIPS - way_z, Z_CHIPS), x, core)
     y_up = (index, lax.rem(y + 1, 4))
     y_down = (index, lax.rem(y + 3, 4))
 
@@ -71,64 +74,64 @@
         )
 
     barrier = pltpu.get_barrier_semaphore()
-    for other in (z_up, z_down, x_up, x_down, sibling, partner, y_up, y_down):
+    for other in (z_up, z_down, x_up, x_down, sibling, onward, behind, y_up, y_down):
         pl.semaphore_signal(barrier, inc=1, device_id=other, device_id_type=MESH)
-    pl.semaphore_wait(barrier, 8)
-
-    def part(ref, half):
-        return ref.at[pl.ds(half * 256, 256), :]
-
-    def send(source, slot, half, target):
+    pl.semaphore_wait(barrier, 9)
+
+    def part(ref, q):
+        return ref.at[pl.ds(q * QUARTER, QUARTER), :]
+
+    def send(source, slot, q, target):
         return pltpu.make_async_remote_copy(
-            src_ref=part(win.at[source], half),
-            dst_ref=part(win.at[slot], half),
-            send_sem=kv_send.at[slot, half],
-            recv_sem=kv_recv.at[slot, half],
+            src_ref=part(win.at[source], q),
+            dst_ref=part(win.at[slot], q),
+            send_sem=kv_send.at[slot, q],
+            recv_sem=kv_recv.at[slot, q],
             device_id=target,
             device_id_type=MESH,
         )
 
-    def send_relay(source, half, way, target):
+    def send_relay(source, q, target):
         return pltpu.make_async_remote_copy(
-            src_ref=part(win.at[source], half),
-            dst_ref=relay.at[way],
-            send_sem=kv_send.at[9, way],
-            recv_sem=kv_recv.at[9, way],
+            src_ref=part(win.at[source], q),
+            dst_ref=relay.at[q],
+            send_sem=kv_send.at[9, q],
+            recv_sem=kv_recv.at[9, q],
             device_id=target,
             device_id_type=MESH,
         )
 
-    def pass_relay(half, way, target):
+    def hand_over(q, target):
         return pltpu.make_async_remote_copy(
-            src_ref=relay.at[way],
-            dst_ref=part(win.at[MID], half),
-            send_sem=kv_send.at[MID, half],
-            recv_sem=kv_recv.at[MID, half],
+            src_ref=relay.at[q],
+            dst_ref=part(win.at[MID], q),
+            send_sem=kv_send.at[10, q],
+            recv_sem=kv_recv.at[MID, q],
             device_id=target,
             device_id_type=MESH,
         )
 
+    def pass_relay(q, target):
+        send_relay(OWN, q, target).wait_recv()
+        hand_over(q, target).start()
+
     load_k.wait()
     load_v.wait()
 
-    for half in (0, 1):
-        send(OWN, ABOVE, half, z_up).start()
+    for q in range(4):
+        send(OWN, ABOVE, q, z_up).start()
 
         @pl.when(x < 3)
         def _():
-            send(OWN, NEAR, half, x_up).start()
+            send(OWN, NEAR, q, x_up).start()
 
         @pl.when(x == 0)
         def _():
-            send(OWN, FAR, half, x_down).start()
+            send(OWN, FAR, q, x_down).start()
 
         @pl.when(core == 0)
         def _():
-            send(OWN, CROSS, half, sibling).start()
-
-    @pl.when(x == 1)
-    def _():
-        send_relay(OWN, 1, 1, x_down).start()
+            send(OWN, CROSS, q, sibling).start()
 
     for copy in load_w:
         copy.start()
@@ -164,12 +167,17 @@
     m_ref[...] = jnp.full(m_ref.shape, -3e38, F32)
     acc[...] = jnp.zeros(acc.shape, F32)
 
-    def prepare(tile, base):
-        hot = jnp.where(same_doc(base, T), 1.0, 0.0).astype(BF16)
-        for g in range(KV):
-            ka[2 * tile + g, :, :HEAD_DIM] = win[tile, :, g * HEAD_DIM : (g + 1) * HEAD_DIM]
-            ka[2 * tile + g, :, HEAD_DIM:] = hot
-            vat[2 * tile + g, :HEAD_DIM, :] = transposed(win[tile, :, 256 + g * HEAD_DIM : 256 + (g + 1) * HEAD_DIM])
+    def prepare(tile, parts):
+        for spot, (slot, start, base) in enumerate(parts):
+            keys = pl.ds(spot * 256, 256)
+            rows = pl.ds(start, 256)
+            hot = jnp.where(same_doc(base, 256), 1.0, 0.0).astype(BF16)
+            for g in range(KV):
+                ka[2 * tile + g, keys, :HEAD_DIM] = win[slot, rows, g * HEAD_DIM : (g + 1) * HEAD_DIM]
+                ka[2 * tile + g, keys, HEAD_DIM:] = hot
+                vat[2 * tile + g, :HEAD_DIM, keys] = transposed(
+                    win[slot, rows, 256 + g * HEAD_DIM : 256 + (g + 1) * HEAD_DIM]
+                )
 
     scores, probs, scales = (s0, s1), (p0, p1), (a0, a1)
 
@@ -190,7 +198,7 @@
     def weigh(kg, c, which):
         acc[c] = acc[c] * scales[which][...] + jnp.dot(vat[kg], probs[which][...], preferred_element_type=F32)
 
-    prepare(OWN, index * T)
+    prepare(OWN, ((OWN, 0, index * T), (OWN, 256, index * T + 256)))
     lanes = lax.broadcasted_iota(jnp.int32, (T, T), 1)
     key_row = lax.broadcasted_iota(jnp.int32, (T, T), 0)
     inner = lanes % BLOCK
@@ -204,66 +212,63 @@
             soften(half * 4 + u, u % 2)
             weigh(u // 2, half * 4 + u, u % 2)
 
+    def above_came(q):
+        send(OWN, ABOVE, q, z_up).wait_recv()
+
+        @pl.when(x > 0)
+        def _():
+            send(ABOVE, FAR, q, x_down).start()
+
+        @pl.when(x == 3)
+        def _():
+            send(ABOVE, NEAR, q, x_up).start()
+
+        @pl.when(core == 1)
+        def _():
+            send(ABOVE, CROSS, q, sibling).start()
+
+    def near_came(q):
+        send(OWN, NEAR, q, x_up).wait_recv()
+        send(NEAR, NEAR_O, q, sibling).start()
+        if q < 2:
+
+            @pl.when(x != 3)
+            def _():
+                send(NEAR, MID, q, x_up).start()
+
+            @pl.when(x == 3)
+            def _():
+                send_relay(NEAR, q, x_up).start()
+
+    def far_came(q):
+        send(OWN, FAR, q, x_down).wait_recv()
+        send(FAR, FAR_O, q, sibling).start()
+        if q >= 2:
+
+            @pl.when(x != 0)
+            def _():
+                send(FAR, MID, q, x_down).start()
+
+            @pl.when(x == 0)
+            def _():
+                send_relay(FAR, q, x_down).start()
+
+    def mid_came(q):
+        send(OWN, MID, q, x_up).wait_recv()
+        send(MID, MID_O, q, sibling).start()
+
+    def came(slot, *quarters):
+        for q in quarters:
+            send(OWN, slot, q, sibling).wait_recv()
+
     own_half(0)
-    own_half(1)
-
-    for half in (0, 1):
-        send(OWN, ABOVE, half, z_up).wait_recv()
-
-        @pl.when(x == 2)
-        def _():
-            if half == 0:
-                send_relay(ABOVE, 0, 0, x_up).start()
-
-        @pl.when(x > 0)
-        def _():
-            send(ABOVE, FAR, half, x_down).start()
-
-        @pl.when(x == 3)
-        def _():
-            send(ABOVE, NEAR, half, x_up).start()
-
-        @pl.when(core == 1)
-        def _():
-            send(ABOVE, CROSS, half, sibling).start()
-
-    @pl.when(x == 0)
-    def _():
-        send_relay(OWN, 1, 1, x_down).wait_recv()
-        pass_relay(1, 1, x_down).start()
-
-    def near_came():
-        for half in (0, 1):
-            send(OWN, NEAR, half, x_up).wait_recv()
-            send(NEAR, NEAR_O, half, sibling).start()
-            if half == 0:
-
-                @pl.when(x != 3)
-                def _():
-                    send(NEAR, MID, 0, x_up).start()
+    above_came(0)
 
     @pl.when(x != 0)
     def _():
-        near_came()
-
-    def came(slot):
-        for half in (0, 1):
-            send(OWN, slot, half, sibling).wait_recv()
-
-    def far_came():
-        for half in (0, 1):
-            send(OWN, FAR, half, x_down).wait_recv()
-            send(FAR, FAR_O, half, sibling).start()
-            if half == 1:
-
-                @pl.when(x != 0)
-                def _():
-                    send(FAR, MID, 1, x_down).start()
-
-    def mid_came():
-        for half in (0, 1):
-            send(OWN, MID, half, x_up).wait_recv()
-            send(MID, MID_O, half, sibling).start()
+        near_came(0)
+
+    own_half(1)
 
     def copy_y(kind, block, way):
         return pltpu.make_async_remote_copy(
@@ -284,9 +289,11 @@
             att[block], wbuf[step, :, part_index * HALF : (part_index + 1) * HALF], preferred_element_type=F32
         )
 
-    def first_step(block):
+    def start_sum(block):
         for way in (0, 1):
             give(0, block, way, project(block, 2, way))
+
+    def own_part(block):
         give(1, block, 0, project(block, 1, 1))
         give(1, block, 1, project(block, 3, 0))
         keep[block, 0] = project(block, 1, 0)
@@ -305,13 +312,13 @@
         right = own[1] + landed[1, block, 0].astype(F32) + landed[2, block, 1].astype(F32)
         return left.astype(BF16), right.astype(BF16)
 
-    def copy_z(block):
+    def copy_z(leg, block):
         return pltpu.make_async_remote_copy(
-            src_ref=res.at[block],
-            dst_ref=moved_in.at[block],
-            send_sem=z_send.at[block],
-            recv_sem=z_recv.at[block],
-            device_id=partner,
+            src_ref=res.at[block] if leg == 0 else midway.at[block],
+            dst_ref=midway.at[block] if leg == 0 else moved_in.at[block],
+            send_sem=z_send.at[leg, block],
+            recv_sem=z_recv.at[leg, block],
+            device_id=onward,
             device_id_type=MESH,
         )
 
@@ -319,7 +326,11 @@
         left, right = last_step(block)
         res[block, :, :HALF] = left
         res[block, :, HALF:] = right
-        copy_z(block).start()
+        copy_z(0, block).start()
+
+    def carry_moved(block):
+        copy_z(0, block).wait_recv()
+        copy_z(1, block).start()
 
     def finish_kept(block):
         left, right = last_step(block)
@@ -337,19 +348,29 @@
                     start = r * 256 + b * BLOCK
                     att[half * 2 + b, :, h * HEAD_DIM : (h + 1) * HEAD_DIM] = rows[start : start + BLOCK]
 
-    back = (0, 1, 1, 3, 3, 2, 2)
-
     def run_half(half, hooks):
         def segment(s, carry):
             tile = s + 1
             for when, hook in hooks.items():
                 pl.when(s == when)(hook)
             if half == 0:
-                distance = jnp.where(tile >= MID, 2, jnp.where(tile >= FAR, 3, 1))
-                side = jnp.where(lax.rem(tile, 2) == 0, core, 1 - core)
-                distance = jnp.where(tile == CROSS, jnp.where(core == 0, 4, 0), distance)
-                there = lax.rem(chip - distance + CHIPS, CHIPS)
-                prepare(tile, (there * 2 + side) * T)
+                cross = tile == 3
+                slot = jnp.where(cross, CROSS, jnp.where(tile >= 6, MID, jnp.where(lax.rem(tile, 3) == 1, NEAR, FAR)))
+                distance = jnp.where(slot == MID, 2, jnp.where(slot == FAR, 3, 1))
+                distance = jnp.where(cross, jnp.where(core == 0, 4, 0), distance)
+                high = jnp.where(tile == 4, 1, jnp.where(tile == 5, 1, jnp.where(tile == 7, 1, 0)))
+                there = 2 * lax.rem(chip - distance + CHIPS, CHIPS)
+                start0 = pl.multiple_of(high * 256, 256)
+                start1 = pl.multiple_of(jnp.where(cross, 256, high * 256), 256)
+                slot1 = jnp.where(cross, CROSS, slot + 1)
+                side0 = jnp.where(cross, 1 - core, core)
+                prepare(
+                    tile,
+                    (
+                        (slot, start0, (there + side0) * T + start0),
+                        (slot1, start1, (there + 1 - core) * T + start1),
+                    ),
+                )
             first = s == 0
             for u in range(4):
                 c = half * 4 + u
@@ -366,69 +387,133 @@
         weigh(15, half * 4 + 2, 0)
         weigh(15, half * 4 + 3, 1)
 
-    def hook_near():
-        pl.when(x == 0)(near_came)
-
-    def hook_near_other():
-        came(NEAR_O)
-
+    def before_near_low():
+        above_came(1)
+
+        @pl.when(x == 0)
+        def _():
+            near_came(0)
+
+        near_came(1)
+        came(NEAR_O, 0, 1)
+
+    def before_far_low():
+        above_came(2)
+        far_came(0)
+
+        @pl.when(x != 0)
+        def _():
+            near_came(2)
+
+        far_came(1)
+        came(FAR_O, 0, 1)
+
+    def before_cross():
+        above_came(3)
+
+        @pl.when(x == 0)
+        def _():
+            pass_relay(0, z_up)
+            pass_relay(1, z_up)
+
+        far_came(2)
+
+        @pl.when(x != 0)
+        def _():
+            near_came(3)
+
+        came(CROSS, 0, 1, 2, 3)
+
+    def before_near_high():
+        @pl.when(x == 0)
+        def _():
+            near_came(2)
+            near_came(3)
+
+        far_came(3)
+        came(NEAR_O, 2, 3)
+
+    def before_far_high():
         @pl.when(x == 3)
         def _():
-            send_relay(OWN, 0, 0, x_up).wait_recv()
-            pass_relay(0, 0, x_up).start()
-
-        far_came()
+            pass_relay(2, z_down)
+
+        came(FAR_O, 2, 3)
+
+    def before_mid_low():
+        @pl.when(x == 3)
+        def _():
+            pass_relay(3, z_down)
+
+        mid_came(0)
+        mid_came(1)
+        came(MID_O, 0, 1)
+
+    def before_mid_high():
+        mid_came(2)
+        mid_came(3)
+        came(MID_O, 2, 3)
 
     run_half(
         0,
         {
-            0: lambda: came(CROSS),
-            1: hook_near,
-            2: hook_near_other,
-            4: lambda: came(FAR_O),
-            5: mid_came,
-            6: lambda: came(MID_O),
+            0: before_near_low,
+            1: before_far_low,
+            2: before_cross,
+            3: before_near_high,
+            4: before_far_high,
+            5: before_mid_low,
+            6: before_mid_high,
         },
     )
     normalise(0)
     for copy in load_w:
         copy.wait()
-    first_step(0)
-    first_step(1)
+    start_sum(0)
+    own_part(0)
+    start_sum(1)
+    second_step(0)
+    own_part(1)
     run_half(
         1,
-        {0: lambda: second_step(0), 2: lambda: second_step(1), 5: lambda: finish_moved(0)},
+        {1: lambda: second_step(1), 4: lambda: finish_moved(0)},
     )
     normalise(1)
-    first_step(2)
-    first_step(3)
+    start_sum(2)
+    own_part(2)
+    start_sum(3)
     finish_moved(1)
+    carry_moved(0)
+    own_part(3)
     second_step(2)
     second_step(3)
+    carry_moved(1)
     finish_kept(2)
     finish_kept(3)
     for block in (0, 1):
-        copy_z(block).wait_recv()
+        copy_z(1, block).wait_recv()
         out[pl.ds((2 + block) * BLOCK, BLOCK), :] = moved_in[block]
 
-    for half in (0, 1):
-        for slot in (ABOVE, CROSS, NEAR, NEAR_O, FAR, FAR_O, MID, MID_O):
-            send(OWN, slot, half, sibling).wait_send()
-
-    @pl.when(x == 1)
-    def _():
-        send_relay(OWN, 1, 1, x_down).wait_send()
-
-    @pl.when(x == 2)
-    def _():
-        send_relay(ABOVE, 0, 0, x_up).wait_send()
+    for q in range(4):
+        for slot in (ABOVE, CROSS, NEAR, NEAR_O, FAR, FAR_O, MID_O):
+            send(OWN, slot, q, sibling).wait_send()
+
+    for q in (0, 1):
+        pl.when(x != 3)(send(NEAR, MID, q, x_up).wait_send)
+        pl.when(x == 3)(send_relay(NEAR, q, x_up).wait_send)
+        pl.when(x == 0)(hand_over(q, z_up).wait_send)
+    for q in (2, 3):
+        pl.when(x != 0)(send(FAR, MID, q, x_down).wait_send)
+        pl.when(x == 0)(send_relay(FAR, q, x_down).wait_send)
+        pl.when(x == 3)(hand_over(q, z_down).wait_send)
 
     for block in range(4):
         for kind in range(3):
             for way in (0, 1):
                 copy_y(kind, block, way).wait_send()
     for block in (0, 1):
-        copy_z(block).wait_send()
+        for leg in (0, 1):
+            copy_z(leg, block).wait_send()
 
 
 def local(queries, key_rows, value_rows, doc_lengths, block_plan, out_weight):
@@ -443,7 +528,7 @@
         scratch_shapes=[
             pltpu.VMEM((4, BLOCK, width), BF16),
             pltpu.VMEM((9, T, 512), BF16),
-            pltpu.VMEM((2, 256, 512), BF16),
+            pltpu.VMEM((4, QUARTER, 512), BF16),
             pltpu.VMEM((4, WIDE, WIDE), BF16),
             pltpu.VMEM((16, T, 256), BF16),
             pltpu.VMEM((16, VROWS, T), BF16),
@@ -462,14 +547,15 @@
             pltpu.VMEM((3, 4, 2, BLOCK, HALF), BF16),
             pltpu.VMEM((2, BLOCK, WIDE), BF16),
             pltpu.VMEM((2, BLOCK, WIDE), BF16),
+            pltpu.VMEM((2, BLOCK, WIDE), BF16),
             pltpu.SemaphoreType.DMA((3,)),
             pltpu.SemaphoreType.DMA((4,)),
-            pltpu.SemaphoreType.DMA((10, 2)),
-            pltpu.SemaphoreType.DMA((10, 2)),
+            pltpu.SemaphoreType.DMA((11, 4)),
+            pltpu.SemaphoreType.DMA((11, 4)),
             pltpu.SemaphoreType.DMA((3, 4, 2)),
             pltpu.SemaphoreType.DMA((3, 4, 2)),
-            pltpu.SemaphoreType.DMA((2,)),
-            pltpu.SemaphoreType.DMA((2,)),
+            pltpu.SemaphoreType.DMA((2, 2)),
+            pltpu.SemaphoreType.DMA((2, 2)),
         ],
         compiler_params=pltpu.CompilerParams(
             collective_id=0, has_side_effects=True, vmem_limit_bytes=56 << 20

time: 91.3 us -> 94.8 us (1.038)
  Pallas kernels: 88.8 us -> 92 us
    pallas_call x1, Pallas kernels: 88.8 us -> 92 us  [local(): pl.pallas_call(kernel, out_shape=jax.ShapeDtypeStruct((tokens, width), BF...]
where the time goes in v2:
time: 94.8 us; the launch traced here: 94.2 us
  Pallas kernels  92 us (97%)
  local copies, waits for them, and re-layouts  2.26 us (2%)
    pallas_call x1, Pallas kernels, local(): pl.pallas_call(kernel, out_shape=jax.ShapeDtypeStruct((tokens, width), BF...  92 us
    unnamed x1, local copies, waits for them, and re-layouts  2.26 us

profile of v2, /device:TPU:1, one launch (start us, length us, event | category | flops | bytes accessed | tf_op | source)
XLA Modules:
  0.0 94.2 jit_solution(18171300987018235788)
XLA Ops:
  0.0 92.0 %attend_and_project.1 = bf16[512,1024]{1,0:T(8,128)(2,1)} custom-call(bf16[4,128,1024]{2,1,0:T(8,128)(2,1)} %bitcast.1, bf16[512,256]{1,0:T(8,128)(2,1)} %k_hbm.1, bf16[512,256]{1,0:T(8,128)(2,1)} %v_hbm.1, s32[64]{0:T(128)} %lens.1, s32[4]{0:T(128)} %plan.1, bf16[1024,4096]{1,0:T(8,128)(2,1)} %w_hbm.1), custom_call_target="tpu_custom_call" | custom-call | tf_op jit(solution)/shard_map/attend_and_project/pallas_call | solution.py:523
  92.0 2.3 %copy.8 = bf16[512,1024]{1,0:T(8,128)(2,1)} copy(bf16[512,1024]{1,0:T(8,128)(2,1)} %attend_and_project.1) | data formatting | bytes 2097152

commit v3 on v1

--- a/solution.py
+++ b/solution.py
@@ -150,8 +150,11 @@
         pos = base + lax.broadcasted_iota(jnp.int32, (rows, HEAD_DIM), 0)
         return jnp.logical_and(pos >= begins, pos < ends)
 
-    for g in range(2 * 8):
-        vat[g, HEAD_DIM:, :] = jnp.ones((VROWS - HEAD_DIM, T), BF16)
+    for g in range(KV):
+        vat[g, HEAD_DIM:, :] = jnp.ones((VROWS - HEAD_DIM, 8 * T), BF16)
+    s1[...] = jnp.zeros(s1.shape, F32)
+    p0[...] = jnp.zeros(p0.shape, BF16)
+    a0[...] = jnp.zeros(a0.shape, F32)
     load_q.wait()
     for b in range(4):
         rows = qv[ids[b]]
@@ -166,29 +169,40 @@
 
     def prepare(tile, base):
         hot = jnp.where(same_doc(base, T), 1.0, 0.0).astype(BF16)
+        keys = slice(tile * T, (tile + 1) * T)
         for g in range(KV):
-            ka[2 * tile + g, :, :HEAD_DIM] = win[tile, :, g * HEAD_DIM : (g + 1) * HEAD_DIM]
-            ka[2 * tile + g, :, HEAD_DIM:] = hot
-            vat[2 * tile + g, :HEAD_DIM, :] = transposed(win[tile, :, 256 + g * HEAD_DIM : 256 + (g + 1) * HEAD_DIM])
+            ka[g, keys, :HEAD_DIM] = win[tile, :, g * HEAD_DIM : (g + 1) * HEAD_DIM]
+            ka[g, keys, HEAD_DIM:] = hot
+            vat[g, :HEAD_DIM, keys] = transposed(win[tile, :, 256 + g * HEAD_DIM : 256 + (g + 1) * HEAD_DIM])
+
+    def prepare_pair(tile, distance):
+        there = 2 * lax.rem(chip - distance + CHIPS, CHIPS)
+        prepare(tile, (there + core) * T)
+        prepare(tile + 1, (there + 1 - core) * T)
 
     scores, probs, scales = (s0, s1), (p0, p1), (a0, a1)
 
-    def score(kg, c, which, causal):
-        value = jnp.dot(ka[kg], qt[c], preferred_element_type=F32)
+    def keys_at(start, count):
+        return pl.ds(start if isinstance(start, int) else pl.multiple_of(start, 256), count)
+
+    def score(g, start, count, c, which, causal):
+        value = jnp.dot(ka[g, keys_at(start, count), :], qt[c], preferred_element_type=F32)
         if causal is not None:
             value = jnp.where(causal, value, -BIG)
-        scores[which][...] = value
-
-    def soften(c, which):
-        value = scores[which][...]
+        scores[which][:count] = value
+
+    def soften(count, c, which):
+        value = scores[which][:count]
         old = m_ref[c]
         new = jnp.maximum(old, jnp.max(value, axis=0, keepdims=True))
-        probs[which][...] = jnp.exp2((value - new) * EXP_SCALE).astype(BF16)
+        probs[which][:count] = jnp.exp2((value - new) * EXP_SCALE).astype(BF16)
         scales[which][...] = jnp.exp2((old - new) * EXP_SCALE)
         m_ref[c] = new
 
-    def weigh(kg, c, which):
-        acc[c] = acc[c] * scales[which][...] + jnp.dot(vat[kg], probs[which][...], preferred_element_type=F32)
+    def weigh(g, start, count, c, which):
+        acc[c] = acc[c] * scales[which][...] + jnp.dot(
+            vat[g, :, keys_at(start, count)], probs[which][:count], preferred_element_type=F32
+        )
 
     prepare(OWN, index * T)
     lanes = lax.broadcasted_iota(jnp.int32, (T, T), 1)
@@ -200,9 +214,9 @@
     def own_half(half):
         causal = key_row <= limits[half]
         for u in range(4):
-            score(u // 2, half * 4 + u, u % 2, causal)
-            soften(half * 4 + u, u % 2)
-            weigh(u // 2, half * 4 + u, u % 2)
+            score(u // 2, 0, T, half * 4 + u, u % 2, causal)
+            soften(T, half * 4 + u, u % 2)
+            weigh(u // 2, 0, T, half * 4 + u, u % 2)
 
     own_half(0)
     own_half(1)
@@ -284,9 +298,11 @@
             att[block], wbuf[step, :, part_index * HALF : (part_index + 1) * HALF], preferred_element_type=F32
         )
 
-    def first_step(block):
+    def start_sum(block):
         for way in (0, 1):
             give(0, block, way, project(block, 2, way))
+
+    def own_part(block):
         give(1, block, 0, project(block, 1, 1))
         give(1, block, 1, project(block, 3, 0))
         keep[block, 0] = project(block, 1, 0)
@@ -337,73 +353,79 @@
                     start = r * 256 + b * BLOCK
                     att[half * 2 + b, :, h * HEAD_DIM : (h + 1) * HEAD_DIM] = rows[start : start + BLOCK]
 
-    back = (0, 1, 1, 3, 3, 2, 2)
-
-    def run_half(half, hooks):
+    def run_half(half, begin, count, segments, hooks):
         def segment(s, carry):
-            tile = s + 1
             for when, hook in hooks.items():
                 pl.when(s == when)(hook)
-            if half == 0:
-                distance = jnp.where(tile >= MID, 2, jnp.where(tile >= FAR, 3, 1))
-                side = jnp.where(lax.rem(tile, 2) == 0, core, 1 - core)
-                distance = jnp.where(tile == CROSS, jnp.where(core == 0, 4, 0), distance)
-                there = lax.rem(chip - distance + CHIPS, CHIPS)
-                prepare(tile, (there * 2 + side) * T)
             first = s == 0
+            start = begin + s * count
+            before = jnp.where(first, start, start - count)
             for u in range(4):
                 c = half * 4 + u
-                score(2 * tile + u // 2, c, u % 2, None)
-                soften(c - 1 if u else jnp.where(first, DUMMY, half * 4 + 3), (u + 1) % 2)
+                score(u // 2, start, count, c, u % 2, None)
+                soften(count, c - 1 if u else jnp.where(first, DUMMY, half * 4 + 3), (u + 1) % 2)
                 if u >= 2:
-                    weigh(2 * tile + (u - 2) // 2, c - 2, u % 2)
+                    weigh((u - 2) // 2, start, count, c - 2, u % 2)
                 else:
-                    weigh(2 * s + 1, jnp.where(first, DUMMY, half * 4 + 2 + u), u % 2)
+                    weigh(1, before, count, jnp.where(first, DUMMY, half * 4 + 2 + u), u % 2)
             return carry
 
-        lax.fori_loop(0, 7, segment, 0)
-        soften(half * 4 + 3, 1)
-        weigh(15, half * 4 + 2, 0)
-        weigh(15, half * 4 + 3, 1)
-
-    def hook_near():
+        lax.fori_loop(0, segments, segment, 0)
+        last = begin + (segments - 1) * count
+        soften(count, half * 4 + 3, 1)
+        weigh(1, last, count, half * 4 + 2, 0)
+        weigh(1, last, count, half * 4 + 3, 1)
+
+    came(CROSS)
+    prepare(CROSS, (2 * lax.rem(chip + CHIPS - jnp.where(core == 0, 4, 0), CHIPS) + 1 - core) * T)
+    for u in range(4):
+        score(u // 2, T, T, u, u % 2, None)
+        soften(T, u, u % 2)
+        weigh(u // 2, T, T, u, u % 2)
+
+    def before_near():
         pl.when(x == 0)(near_came)
-
-    def hook_near_other():
         came(NEAR_O)
+        prepare_pair(NEAR, 1)
+
+    def before_far():
+        far_came()
 
         @pl.when(x == 3)
         def _():
             send_relay(OWN, 0, 0, x_up).wait_recv()
             pass_relay(0, 0, x_up).start()
 
-        far_came()
-
-    run_half(
-        0,
-        {
-            0: lambda: came(CROSS),
-            1: hook_near,
-            2: hook_near_other,
-            4: lambda: came(FAR_O),
-            5: mid_came,
-            6: lambda: came(MID_O),
-        },
-    )
+        came(FAR_O)
+        prepare_pair(FAR, 3)
+
+    def before_mid():
+        mid_came()
+        came(MID_O)
+        prepare_pair(MID, 2)
+
+    run_half(0, 2 * T, 2 * T, 3, {0: before_near, 1: before_far, 2: before_mid})
     normalise(0)
     for copy in load_w:
         copy.wait()
-    first_step(0)
-    first_step(1)
-    run_half(
-        1,
-        {0: lambda: second_step(0), 2: lambda: second_step(1), 5: lambda: finish_moved(0)},
-    )
+    start_sum(0)
+    own_part(0)
+    start_sum(1)
+    second_step(0)
+    own_part(1)
+
+    def between():
+        second_step(1)
+        finish_moved(0)
+
+    run_half(1, T, 7 * T // 2, 2, {1: between})
     normalise(1)
-    first_step(2)
-    first_step(3)
+    start_sum(2)
+    own_part(2)
+    start_sum(3)
     finish_moved(1)
     second_step(2)
+    own_part(3)
     second_step(3)
     finish_kept(2)
     finish_kept(3)
@@ -445,15 +467,15 @@
             pltpu.VMEM((9, T, 512), BF16),
             pltpu.VMEM((2, 256, 512), BF16),
             pltpu.VMEM((4, WIDE, WIDE), BF16),
-            pltpu.VMEM((16, T, 256), BF16),
-            pltpu.VMEM((16, VROWS, T), BF16),
+            pltpu.VMEM((KV, 8 * T, 256), BF16),
+            pltpu.VMEM((KV, VROWS, 8 * T), BF16),
             pltpu.VMEM((8, 256, T), BF16),
             pltpu.VMEM((9, 1, T), F32),
             pltpu.VMEM((9, VROWS, T), F32),
-            pltpu.VMEM((T, T), F32),
-            pltpu.VMEM((T, T), F32),
-            pltpu.VMEM((T, T), BF16),
-            pltpu.VMEM((T, T), BF16),
+            pltpu.VMEM((7 * T // 2, T), F32),
+            pltpu.VMEM((7 * T // 2, T), F32),
+            pltpu.VMEM((7 * T // 2, T), BF16),
+            pltpu.VMEM((7 * T // 2, T), BF16),
             pltpu.VMEM((1, T), F32),
             pltpu.VMEM((1, T), F32),
             pltpu.VMEM((4, BLOCK, WIDE), BF16),

time: 91.3 us -> 91.7 us (level)
  no operation moved by 1% of the time
where the time goes in v3:
time: 91.7 us; the launch traced here: 91.5 us
  Pallas kernels  89.3 us (97%)
  local copies, waits for them, and re-layouts  2.26 us (2%)
    pallas_call x1, Pallas kernels, local(): pl.pallas_call(kernel, out_shape=jax.ShapeDtypeStruct((tokens, width), BF...  89.3 us
    unnamed x1, local copies, waits for them, and re-layouts  2.26 us

profile of v3, /device:TPU:1, one launch (start us, length us, event | category | flops | bytes accessed | tf_op | source)
XLA Modules:
  0.0 91.5 jit_solution(9685952598695658853)
XLA Ops:
  0.0 89.3 %attend_and_project.1 = bf16[512,1024]{1,0:T(8,128)(2,1)} custom-call(bf16[4,128,1024]{2,1,0:T(8,128)(2,1)} %bitcast.1, bf16[512,256]{1,0:T(8,128)(2,1)} %k_hbm.1, bf16[512,256]{1,0:T(8,128)(2,1)} %v_hbm.1, s32[64]{0:T(128)} %lens.1, s32[4]{0:T(128)} %plan.1, bf16[1024,4096]{1,0:T(8,128)(2,1)} %w_hbm.1), custom_call_target="tpu_custom_call" | custom-call | tf_op jit(solution)/shard_map/attend_and_project/pallas_call | solution.py:460
  89.3 2.3 %copy.8 = bf16[512,1024]{1,0:T(8,128)(2,1)} copy(bf16[512,1024]{1,0:T(8,128)(2,1)} %attend_and_project.1) | data formatting | bytes 2097152

commit v4 on v3

--- a/solution.py
+++ b/solution.py
@@ -17,6 +17,7 @@
 KV = 2
 T = 512
 BLOCK = 128
+QUARTER = 128
 WIDE = 1024
 HALF = 512
 VROWS = HEAD_DIM + 16
@@ -75,60 +76,50 @@
         pl.semaphore_signal(barrier, inc=1, device_id=other, device_id_type=MESH)
     pl.semaphore_wait(barrier, 8)
 
-    def part(ref, half):
-        return ref.at[pl.ds(half * 256, 256), :]
-
-    def send(source, slot, half, target):
+    def part(ref, q):
+        return ref.at[pl.ds(q * QUARTER, QUARTER), :]
+
+    def send(source, slot, q, target):
         return pltpu.make_async_remote_copy(
-            src_ref=part(win.at[source], half),
-            dst_ref=part(win.at[slot], half),
-            send_sem=kv_send.at[slot, half],
-            recv_sem=kv_recv.at[slot, half],
+            src_ref=part(win.at[source], q),
+            dst_ref=part(win.at[slot], q),
+            send_sem=kv_send.at[slot, q],
+            recv_sem=kv_recv.at[slot, q],
             device_id=target,
             device_id_type=MESH,
         )
 
-    def send_relay(source, half, way, target):
+    def send_relay(source, q, target):
         return pltpu.make_async_remote_copy(
-            src_ref=part(win.at[source], half),
-            dst_ref=relay.at[way],
-            send_sem=kv_send.at[9, way],
-            recv_sem=kv_recv.at[9, way],
+            src_ref=part(win.at[source], q),
+            dst_ref=relay.at[q],
+            send_sem=kv_send.at[9, q],
+            recv_sem=kv_recv.at[9, q],
             device_id=target,
             device_id_type=MESH,
         )
 
-    def pass_relay(half, way, target):
-        return pltpu.make_async_remote_copy(
-            src_ref=relay.at[way],
-            dst_ref=part(win.at[MID], half),
-            send_sem=kv_send.at[MID, half],
-            recv_sem=kv_recv.at[MID, half],
+    def pass_relay(q, target):
+        send_relay(OWN, q, target).wait_recv()
+        pltpu.make_async_remote_copy(
+            src_ref=relay.at[q],
+            dst_ref=part(win.at[MID], q),
+            send_sem=kv_send.at[MID, q],
+            recv_sem=kv_recv.at[MID, q],
             device_id=target,
             device_id_type=MESH,
-        )
+        ).start()
 
     load_k.wait()
     load_v.wait()
 
-    for half in (0, 1):
-        send(OWN, ABOVE, half, z_up).start()
-
-        @pl.when(x < 3)
-        def _():
-            send(OWN, NEAR, half, x_up).start()
-
-        @pl.when(x == 0)
-        def _():
-            send(OWN, FAR, half, x_down).start()
-
-        @pl.when(core == 0)
-        def _():
-            send(OWN, CROSS, half, sibling).start()
-
-    @pl.when(x == 1)
-    def _():
-        send_relay(OWN, 1, 1, x_down).start()
+    for q in (2, 3):
+        pl.when(x == 1)(send_relay(OWN, q, x_down).start)
+    for q in range(4):
+        send(OWN, ABOVE, q, z_up).start()
+        pl.when(x < 3)(send(OWN, NEAR, q, x_up).start)
+        pl.when(x == 0)(send(OWN, FAR, q, x_down).start)
+        pl.when(core == 0)(send(OWN, CROSS, q, sibling).start)
 
     for copy in load_w:
         copy.start()
@@ -205,7 +196,7 @@
         )
 
     prepare(OWN, index * T)
-    lanes = lax.broadcasted_iota(jnp.int32, (T, T), 1)
+    lanes = lax.broadcasted_iota(jnp.int32, (1, T), 1)
     key_row = lax.broadcasted_iota(jnp.int32, (T, T), 0)
     inner = lanes % BLOCK
     second = (lanes // BLOCK) % 2
@@ -218,66 +209,55 @@
             soften(T, half * 4 + u, u % 2)
             weigh(u // 2, 0, T, half * 4 + u, u % 2)
 
+    def above_came(q):
+        send(OWN, ABOVE, q, z_up).wait_recv()
+        if q < 2:
+            pl.when(x == 2)(send_relay(ABOVE, q, x_up).start)
+        pl.when(x > 0)(send(ABOVE, FAR, q, x_down).start)
+        pl.when(x == 3)(send(ABOVE, NEAR, q, x_up).start)
+        pl.when(core == 1)(send(ABOVE, CROSS, q, sibling).start)
+
+    def near_came(*quarters):
+        for q in quarters:
+            send(OWN, NEAR, q, x_up).wait_recv()
+            if q < 2:
+                pl.when(x != 3)(send(NEAR, MID, q, x_up).start)
+            send(NEAR, NEAR_O, q, sibling).start()
+
+    def far_came(q):
+        send(OWN, FAR, q, x_down).wait_recv()
+        if q >= 2:
+            pl.when(x != 0)(send(FAR, MID, q, x_down).start)
+        send(FAR, FAR_O, q, sibling).start()
+
+    def came(slot):
+        for q in range(4):
+            send(OWN, slot, q, sibling).wait_recv()
+
+    def mid_came():
+        for q in range(4):
+            send(OWN, MID, q, x_up).wait_recv()
+            send(MID, MID_O, q, sibling).start()
+
     own_half(0)
+    above_came(0)
+    pl.when(x != 0)(lambda: near_came(0))
     own_half(1)
-
-    for half in (0, 1):
-        send(OWN, ABOVE, half, z_up).wait_recv()
-
-        @pl.when(x == 2)
-        def _():
-            if half == 0:
-                send_relay(ABOVE, 0, 0, x_up).start()
-
-        @pl.when(x > 0)
-        def _():
-            send(ABOVE, FAR, half, x_down).start()
-
-        @pl.when(x == 3)
-        def _():
-            send(ABOVE, NEAR, half, x_up).start()
-
-        @pl.when(core == 1)
-        def _():
-            send(ABOVE, CROSS, half, sibling).start()
+    above_came(1)
+    pl.when(x != 0)(lambda: near_came(1))
 
     @pl.when(x == 0)
     def _():
-        send_relay(OWN, 1, 1, x_down).wait_recv()
-        pass_relay(1, 1, x_down).start()
-
-    def near_came():
-        for half in (0, 1):
-            send(OWN, NEAR, half, x_up).wait_recv()
-            send(NEAR, NEAR_O, half, sibling).start()
-            if half == 0:
-
-                @pl.when(x != 3)
-                def _():
-                    send(NEAR, MID, 0, x_up).start()
-
-    @pl.when(x != 0)
-    def _():
-        near_came()
-
-    def came(slot):
-        for half in (0, 1):
-            send(OWN, slot, half, sibling).wait_recv()
-
-    def far_came():
-        for half in (0, 1):
-            send(OWN, FAR, half, x_down).wait_recv()
-            send(FAR, FAR_O, half, sibling).start()
-            if half == 1:
-
-                @pl.when(x != 0)
-                def _():
-                    send(FAR, MID, 1, x_down).start()
-
-    def mid_came():
-        for half in (0, 1):
-            send(OWN, MID, half, x_up).wait_recv()
-            send(MID, MID_O, half, sibling).start()
+        for q in (2, 3):
+            pass_relay(q, x_down)
+
+    above_came(2)
+    pl.when(x != 0)(lambda: near_came(2))
+    far_came(0)
+    far_came(1)
+    above_came(3)
+    pl.when(x != 0)(lambda: near_came(3))
+    pl.when(x == 0)(lambda: near_came(0, 1))
 
     def copy_y(kind, block, way):
         return pltpu.make_async_remote_copy(
@@ -384,18 +364,15 @@
         weigh(u // 2, T, T, u, u % 2)
 
     def before_near():
-        pl.when(x == 0)(near_came)
+        far_came(2)
+        pl.when(x == 0)(lambda: near_came(2, 3))
+        pl.when(x == 3)(lambda: pass_relay(0, x_up))
+        far_came(3)
         came(NEAR_O)
         prepare_pair(NEAR, 1)
 
     def before_far():
-        far_came()
-
-        @pl.when(x == 3)
-        def _():
-            send_relay(OWN, 0, 0, x_up).wait_recv()
-            pass_relay(0, 0, x_up).start()
-
+        pl.when(x == 3)(lambda: pass_relay(1, x_up))
         came(FAR_O)
         prepare_pair(FAR, 3)
 
@@ -433,17 +410,10 @@
         copy_z(block).wait_recv()
         out[pl.ds((2 + block) * BLOCK, BLOCK), :] = moved_in[block]
 
-    for half in (0, 1):
+    for q in range(4):
         for slot in (ABOVE, CROSS, NEAR, NEAR_O, FAR, FAR_O, MID, MID_O):
-            send(OWN, slot, half, sibling).wait_send()
-
-    @pl.when(x == 1)
-    def _():
-        send_relay(OWN, 1, 1, x_down).wait_send()
-
-    @pl.when(x == 2)
-    def _():
-        send_relay(ABOVE, 0, 0, x_up).wait_send()
+            send(OWN, slot, q, sibling).wait_send()
+        pl.when(x == (2 if q < 2 else 1))(send_relay(OWN, q, x_up).wait_send)
 
     for block in range(4):
         for kind in range(3):
@@ -459,13 +429,13 @@
     scalars = pl.BlockSpec(memory_space=pltpu.SMEM)
     return pl.pallas_call(
         kernel,
-        out_shape=jax.ShapeDtypeStruct((tokens, width), BF16),
+        out_shape=pltpu.VMEM((tokens, width), BF16),
         in_specs=[anywhere, anywhere, anywhere, scalars, scalars, anywhere],
         out_specs=pl.BlockSpec(memory_space=pltpu.VMEM),
         scratch_shapes=[
             pltpu.VMEM((4, BLOCK, width), BF16),
             pltpu.VMEM((9, T, 512), BF16),
-            pltpu.VMEM((2, 256, 512), BF16),
+            pltpu.VMEM((4, QUARTER, 512), BF16),
             pltpu.VMEM((4, WIDE, WIDE), BF16),
             pltpu.VMEM((KV, 8 * T, 256), BF16),
             pltpu.VMEM((KV, VROWS, 8 * T), BF16),
@@ -486,8 +456,8 @@
             pltpu.VMEM((2, BLOCK, WIDE), BF16),
             pltpu.SemaphoreType.DMA((3,)),
             pltpu.SemaphoreType.DMA((4,)),
-            pltpu.SemaphoreType.DMA((10, 2)),
-            pltpu.SemaphoreType.DMA((10, 2)),
+            pltpu.SemaphoreType.DMA((10, 4)),
+            pltpu.SemaphoreType.DMA((10, 4)),
             pltpu.SemaphoreType.DMA((3, 4, 2)),
             pltpu.SemaphoreType.DMA((3, 4, 2)),
             pltpu.SemaphoreType.DMA((2,)),

time: 91.7 us -> 85.5 us (0.932)
  Pallas kernels: 89.3 us -> 84.4 us
  local copies, waits for them, and re-layouts: 2.26 us -> 0.97 us
    pallas_call x1, Pallas kernels: 89.3 us -> 84.4 us  [local(): pl.pallas_call(kernel, out_shape=pltpu.VMEM((tokens, width), BF16), in_sp...]
    unnamed x1, local copies, waits for them, and re-layouts: 2.26 us -> 0.97 us
where the time goes in v4:
time: 85.5 us; the launch traced here: 85.4 us
  Pallas kernels  84.4 us (99%)
  local copies, waits for them, and re-layouts  0.97 us (1%)
    pallas_call x1, Pallas kernels, local(): pl.pallas_call(kernel, out_shape=pltpu.VMEM((tokens, width), BF16), in_sp...  84.4 us

profile of v4, /device:TPU:1, one launch (start us, length us, event | category | flops | bytes accessed | tf_op | source)
XLA Modules:
  0.0 85.4 jit_solution(2693401240113142028)
XLA Ops:
  0.0 84.4 %attend_and_project.1 = bf16[512,1024]{1,0:T(8,128)(2,1)S(1)} custom-call(bf16[4,128,1024]{2,1,0:T(8,128)(2,1)} %bitcast.1, bf16[512,256]{1,0:T(8,128)(2,1)} %k_hbm.1, bf16[512,256]{1,0:T(8,128)(2,1)} %v_hbm.1, s32[64]{0:T(128)} %lens.1, s32[4]{0:T(128)} %plan.1, bf16[1024,4096]{1,0:T(8,128)(2,1)} %w_hbm.1), custom_call_target="tpu_custom_call" | custom-call | tf_op jit(solution)/shard_map/attend_and_project/pallas_call | solution.py:430
  84.4 1.0 %copy.8 = bf16[512,1024]{1,0:T(8,128)(2,1)} copy(bf16[512,1024]{1,0:T(8,128)(2,1)S(1)} %attend_and_project.1) | data formatting | bytes 2097152

commit v5 on v4

--- a/solution.py
+++ b/solution.py
@@ -234,10 +234,9 @@
         for q in range(4):
             send(OWN, slot, q, sibling).wait_recv()
 
-    def mid_came():
-        for q in range(4):
-            send(OWN, MID, q, x_up).wait_recv()
-            send(MID, MID_O, q, sibling).start()
+    def mid_came(q):
+        send(OWN, MID, q, x_up).wait_recv()
+        send(MID, MID_O, q, sibling).start()
 
     own_half(0)
     above_came(0)
@@ -376,12 +375,27 @@
         came(FAR_O)
         prepare_pair(FAR, 3)
 
-    def before_mid():
-        mid_came()
-        came(MID_O)
-        prepare_pair(MID, 2)
-
-    run_half(0, 2 * T, 2 * T, 3, {0: before_near, 1: before_far, 2: before_mid})
+    def before_mid(high):
+        for q in (2 * high, 2 * high + 1):
+            mid_came(q)
+        there = 2 * lax.rem(chip - 2 + CHIPS, CHIPS)
+        rows = slice(high * 256, high * 256 + 256)
+        for spot, (slot, side) in enumerate(((MID, core), (MID_O, 1 - core))):
+            if spot == 1:
+                for q in (2 * high, 2 * high + 1):
+                    send(OWN, MID_O, q, sibling).wait_recv()
+            first_key = MID * T + high * T + spot * 256
+            keys = slice(first_key, first_key + 256)
+            hot = jnp.where(same_doc((there + side) * T + high * 256, 256), 1.0, 0.0).astype(BF16)
+            for g in range(KV):
+                ka[g, keys, :HEAD_DIM] = win[slot, rows, g * HEAD_DIM : (g + 1) * HEAD_DIM]
+                ka[g, keys, HEAD_DIM:] = hot
+                vat[g, :HEAD_DIM, keys] = transposed(
+                    win[slot, rows, 256 + g * HEAD_DIM : 256 + (g + 1) * HEAD_DIM]
+                )
+
+    run_half(0, 2 * T, 2 * T, 2, {0: before_near, 1: before_far})
+    run_half(0, MID * T, T, 2, {0: lambda: before_mid(0), 1: lambda: before_mid(1)})
     normalise(0)
     for copy in load_w:
         copy.wait()

time: 85.5 us -> 89.2 us (1.043)
  Pallas kernels: 84.4 us -> 88.1 us
    pallas_call x1, Pallas kernels: 84.4 us -> 88.1 us  [local(): pl.pallas_call(kernel, out_shape=pltpu.VMEM((tokens, width), BF16), in_sp...]
where the time goes in v5:
time: 89.2 us; the launch traced here: 89.1 us
  Pallas kernels  88.1 us (99%)
  local copies, waits for them, and re-layouts  0.97 us (1%)
    pallas_call x1, Pallas kernels, local(): pl.pallas_call(kernel, out_shape=pltpu.VMEM((tokens, width), BF16), in_sp...  88.1 us

profile of v5, /device:TPU:1, one launch (start us, length us, event | category | flops | bytes accessed | tf_op | source)
XLA Modules:
  0.0 89.1 jit_solution(11070833054648046711)
XLA Ops:
  0.0 88.1 %attend_and_project.1 = bf16[512,1024]{1,0:T(8,128)(2,1)S(1)} custom-call(bf16[4,128,1024]{2,1,0:T(8,128)(2,1)} %bitcast.1, bf16[512,256]{1,0:T(8,128)(2,1)} %k_hbm.1, bf16[512,256]{1,0:T(8,128)(2,1)} %v_hbm.1, s32[64]{0:T(128)} %lens.1, s32[4]{0:T(128)} %plan.1, bf16[1024,4096]{1,0:T(8,128)(2,1)} %w_hbm.1), custom_call_target="tpu_custom_call" | custom-call | tf_op jit(solution)/shard_map/attend_and_project/pallas_call | solution.py:444
  88.1 1.0 %copy.8 = bf16[512,1024]{1,0:T(8,128)(2,1)} copy(bf16[512,1024]{1,0:T(8,128)(2,1)S(1)} %attend_and_project.1) | data formatting | bytes 2097152
